TPU v7x, 32 devices: a whole 2x2x4 slice. The times are simulated.
32 devices in a mesh: mid: 4 (over y, core), leaf: 8 (over z, x).
Axes of the slice: x: 2, y: 2, z: 4, core: 2. Of those that a mesh axis runs over, the one named last changes fastest.
Arguments:
- queries: bfloat16 [8192, 4096], P(('mid', 'leaf')), may hold values from -128 to 128
- out_grad: bfloat16 [8192, 4096], P(('mid', 'leaf')), may hold values from -6 to 6
- leaf_keys: bfloat16 [8192, 1024], P(('mid', 'leaf')), may hold values from -6 to 6
- leaf_values: bfloat16 [8192, 1024], P(('mid', 'leaf')), may hold values from -6 to 6
- mid_keys: bfloat16 [512, 1024], P(('mid', 'leaf')), may hold values from -6 to 6
- mid_values: bfloat16 [512, 1024], P(('mid', 'leaf')), may hold values from -6 to 6
- root_keys: bfloat16 [64, 1024], P(('mid', 'leaf')), may hold values from -4 to 4
- root_values: bfloat16 [64, 1024], P(('mid', 'leaf')), may hold values from -6 to 6
- mid_len: int32 [4], P('mid'), may hold values from 1 to 128, 384 in all
- leaf_len: int32 [32], P(('mid', 'leaf')), may hold values from 1 to 256, 5120 in all
Outputs:
- query_grad: bfloat16 [8192, 4096], P(('mid', 'leaf'))
- leaf_key_grad: bfloat16 [8192, 1024], P(('mid', 'leaf'))
- leaf_value_grad: bfloat16 [8192, 1024], P(('mid', 'leaf'))
- mid_key_grad: float32 [512, 1024], P(('mid', 'leaf'))
- mid_value_grad: float32 [512, 1024], P(('mid', 'leaf'))
- root_key_grad: float32 [64, 1024], P(('mid', 'leaf'))
- root_value_grad: float32 [64, 1024], P(('mid', 'leaf'))
Inputs may be any that keep to these rules, and one draw needn't show every extreme that they name: `mid_len`: at least one mid branch has all 128 tokens live. `leaf_len`: at least one leaf has all 256 tokens live.
All inputs are finite; a program needn't handle non-finite values. No bound on the sum of `mid_len` or of `leaf_len` on one device may be relied on, other than what follows from the above.
Results may differ from a plain program's by a relative error of at most 0.013.
Values may be sent and summed in bfloat16 or wider, within the bound.
No kernel may reach another device: no remote copies, remote signals or barrier semaphores. Data moves between devices by JAX's collectives and lax.ppermute only.
A program may use at most 128 MiB of HBM per device.

v0:
```python
import jax
import jax.numpy as jnp
from jax import lax
from jax.sharding import PartitionSpec as P

QH = 32
KVH = 8
HD = 128


def leaf_backward(
    queries, out_grad, all_keys, all_values, root_rows, mid_rows, mid_live, leaf_live
):
    leaf_rows = queries.shape[0]
    key_rows = all_keys.shape[0]
    heads_per = QH // KVH
    span_cols = heads_per * HD
    column = jnp.arange(key_rows, dtype=jnp.int32)[None, :]
    row_ids = jnp.arange(leaf_rows, dtype=jnp.int32)[:, None]
    offset = root_rows + mid_rows
    leaf_pos = column - offset
    in_root = column < root_rows
    in_mid = (column >= root_rows) & (column < offset) & (column - root_rows < mid_live)
    in_leaf = (leaf_pos >= 0) & (leaf_pos <= row_ids) & (leaf_pos < leaf_live)
    allowed = in_root | in_mid | in_leaf
    live_rows = (jnp.arange(leaf_rows, dtype=jnp.int32) < leaf_live).astype(jnp.float32)[
        None, :, None
    ]
    factor = HD ** (-0.5)

    def one_head(head_index, buffers):
        query_acc, key_acc, value_acc = buffers
        query_part = lax.dynamic_slice_in_dim(
            queries, head_index * span_cols, span_cols, 1
        ).reshape(leaf_rows, heads_per, HD)
        grad_part = lax.dynamic_slice_in_dim(
            out_grad, head_index * span_cols, span_cols, 1
        ).reshape(leaf_rows, heads_per, HD)
        key_part = lax.dynamic_slice_in_dim(all_keys, head_index * HD, HD, 1)
        value_part = lax.dynamic_slice_in_dim(all_values, head_index * HD, HD, 1)
        scores = factor * jnp.einsum(
            "igd,jd->gij", query_part, key_part, preferred_element_type=jnp.float32
        )
        scores = jnp.where(allowed[None], scores, -1e30)
        row_max = jnp.max(scores, axis=-1, keepdims=True)
        weights = jnp.exp(scores - row_max)
        probs = weights / jnp.sum(weights, axis=-1, keepdims=True) * live_rows
        probs_low = probs.astype(jnp.bfloat16)
        value_term = jnp.einsum(
            "gij,igd->jd", probs_low, grad_part, preferred_element_type=jnp.float32
        )
        dprobs = jnp.einsum(
            "igd,jd->gij", grad_part, value_part, preferred_element_type=jnp.float32
        )
        row_dots = jnp.sum(probs * dprobs, axis=-1, keepdims=True)
        dscores = (probs * (dprobs - row_dots)).astype(jnp.bfloat16)
        query_term = factor * jnp.einsum(
            "gij,jd->igd", dscores, key_part, preferred_element_type=jnp.float32
        )
        key_term = factor * jnp.einsum(
            "gij,igd->jd", dscores, query_part, preferred_element_type=jnp.float32
        )
        query_acc = lax.dynamic_update_slice_in_dim(
            query_acc,
            query_term.reshape(leaf_rows, span_cols).astype(jnp.bfloat16),
            head_index * span_cols,
            1,
        )
        key_acc = lax.dynamic_update_slice_in_dim(key_acc, key_term, head_index * HD, 1)
        value_acc = lax.dynamic_update_slice_in_dim(value_acc, value_term, head_index * HD, 1)
        return (query_acc, key_acc, value_acc)

    start = (
        jnp.zeros((leaf_rows, QH * HD), jnp.bfloat16),
        jnp.zeros((key_rows, KVH * HD), jnp.float32),
        jnp.zeros((key_rows, KVH * HD), jnp.float32),
    )
    return lax.fori_loop(0, KVH, one_head, start)


def on_device(
    queries,
    out_grad,
    leaf_keys,
    leaf_values,
    mid_keys,
    mid_values,
    root_keys,
    root_values,
    mid_len,
    leaf_len,
):
    root_k, root_v = (
        lax.all_gather(root_keys, ("mid", "leaf"), axis=0, tiled=True),
        lax.all_gather(root_values, ("mid", "leaf"), axis=0, tiled=True),
    )
    branch_k, branch_v = (
        lax.all_gather(mid_keys, "leaf", axis=0, tiled=True),
        lax.all_gather(mid_values, "leaf", axis=0, tiled=True),
    )
    root_rows = root_k.shape[0]
    mid_rows = branch_k.shape[0]
    all_keys = jnp.concatenate([root_k, branch_k, leaf_keys], 0)
    all_values = jnp.concatenate([root_v, branch_v, leaf_values], 0)
    query_grad, key_terms, value_terms = leaf_backward(
        queries, out_grad, all_keys, all_values, root_rows, mid_rows, mid_len[0], leaf_len[0]
    )
    offset = root_rows + mid_rows
    leaf_key_grad = key_terms[offset:].astype(jnp.bfloat16)
    leaf_value_grad = value_terms[offset:].astype(jnp.bfloat16)
    root_key_terms = key_terms[:root_rows]
    root_value_terms = value_terms[:root_rows]
    mid_key_terms = key_terms[root_rows:offset]
    mid_value_terms = value_terms[root_rows:offset]
    root_key_grad, root_value_grad = (
        lax.psum_scatter(root_key_terms, ("mid", "leaf"), scatter_dimension=0, tiled=True),
        lax.psum_scatter(root_value_terms, ("mid", "leaf"), scatter_dimension=0, tiled=True),
    )
    mid_key_grad, mid_value_grad = (
        lax.psum_scatter(mid_key_terms, "leaf", scatter_dimension=0, tiled=True),
        lax.psum_scatter(mid_value_terms, "leaf", scatter_dimension=0, tiled=True),
    )
    return (
        query_grad,
        leaf_key_grad,
        leaf_value_grad,
        mid_key_grad,
        mid_value_grad,
        root_key_grad,
        root_value_grad,
    )


def solution(mesh):
    in_specs = (
        P(("mid", "leaf"), None),
        P(("mid", "leaf"), None),
        P(("mid", "leaf"), None),
        P(("mid", "leaf"), None),
        P(("mid", "leaf"), None),
        P(("mid", "leaf"), None),
        P(("mid", "leaf"), None),
        P(("mid", "leaf"), None),
        P("mid"),
        P(("mid", "leaf")),
    )
    out_specs = (
        P(("mid", "leaf"), None),
        P(("mid", "leaf"), None),
        P(("mid", "leaf"), None),
        P(("mid", "leaf"), None),
        P(("mid", "leaf"), None),
        P(("mid", "leaf"), None),
        P(("mid", "leaf"), None),
    )
    return jax.shard_map(
        on_device, mesh=mesh, in_specs=in_specs, out_specs=out_specs, check_vma=False
    )
```

profile of v0, /device:TPU:0, one launch (start us, length us, event | category | flops | bytes accessed | tf_op | source)
XLA Modules:
  0.0 446.1 jit_solution(12240525262746218722)
XLA Ops:
  9.4 32.7 %all_gather.13 = bf16[128,1024]{1,0:T(8,128)(2,1)S(1)} all-gather(bf16[16,1024]{1,0:T(8,128)(2,1)} %param.16), channel_id=1, replica_groups=mesh['mid'=4,'leaf'=8] {'leaf'}, dimensions={0}, use_global_device_ids=true | all-gather | bytes 294912 | tf_op jit(solution)/shard_map/all_gather | solution.py:98
  42.2 65.8 %all-gather = bf16[32,2,1024]{2,1,0:T(2,128)(2,1)S(1)} all-gather(bf16[1,2,1024]{2,1,0:T(2,128)(2,1)} %bitcast.121), channel_id=1, replica_groups=mesh['mid'=4,'leaf'=8] {'mid','leaf'}, dimensions={0}, use_global_device_ids=true | all-gather | bytes 135168 | tf_op jit(solution)/shard_map/all_gather | solution.py:94
  108.0 31.0 %all_gather.15 = bf16[128,1024]{1,0:T(8,128)(2,1)S(1)} all-gather(bf16[16,1024]{1,0:T(8,128)(2,1)} %param.17), channel_id=1, replica_groups=mesh['mid'=4,'leaf'=8] {'leaf'}, dimensions={0}, use_global_device_ids=true | all-gather | bytes 294912 | tf_op jit(solution)/shard_map/all_gather | solution.py:99
  138.9 64.3 %all-gather.1 = bf16[32,2,1024]{2,1,0:T(2,128)(2,1)S(1)} all-gather(bf16[1,2,1024]{2,1,0:T(2,128)(2,1)} %bitcast.122), channel_id=1, replica_groups=mesh['mid'=4,'leaf'=8] {'mid','leaf'}, dimensions={0}, use_global_device_ids=true | all-gather | bytes 135168 | tf_op jit(solution)/shard_map/all_gather | solution.py:95
  203.3 2.0 pad_maximum_fusion
  206.3 1.6 broadcast_in_dim.42.clone
  207.9 1.5 broadcast.97
  209.3 1.5 broadcast.97.clone
  210.8 93.5 %while.18 = (s32[]{:T(128)}, bf16[256,4096]{1,0:T(8,128)(2,1)}, f32[448,1024]{1,0:T(8,128)}, f32[448,1024]{1,0:T(8,128)}, bf16[448,1024]{1,0:T(8,128)(2,1)}, /*i...) while((s32[]{:T(128)}, bf16[256,4096]{1,0:T(8,128)(2,1)}, ...), condition=%wide.region_4.5_spmd.clone, body=%wide.region_0.4_spmd.clone.sunk | while | flops 714139008 | bytes 17940836 | solution.py:78
  212.3 1.7 fusion.92
  219.8 2.8 fusion.97
  224.0 1.7 fusion.92
  231.5 2.7 fusion.97
  235.7 1.7 fusion.92
  243.2 2.7 fusion.97
  247.4 1.7 fusion.92
  254.8 2.7 fusion.97
  259.1 1.7 fusion.92
  266.5 2.7 fusion.97
  270.8 1.7 fusion.92
  278.2 2.7 fusion.97
  282.5 1.7 fusion.92
  289.9 2.8 fusion.97
  294.2 1.7 fusion.92
  301.6 2.7 fusion.97
  304.3 1.8 slice.24
  306.1 1.7 slice.25
  307.9 1.9 slice.22
  311.7 2.1 slice.31
  313.8 121.8 %all-reduce.5.cloned.1.call-done = (f32[64,1024]{1,0:T(8,128)}, f32[64,1024]{1,0:T(8,128)}) async-done(((f32[64,1024]{1,0:T(8,128)}, f32[64,1024]{1,0:T(8,128)}), (f32[64,1024]{1,0:T(8,128)}, f32[64,1024]{1,0:T(8,128)})) %all-reduce.5.cloned.1.call-update) | async-done | bytes 524304
  435.6 1.4 constant_dynamic-slice_fusion.2
  437.0 1.4 constant_dynamic-slice_fusion.3
  (108 shorter events, 61.2 us)
Async XLA Ops:
  8.0 197.3 %copy-start.1 = (bf16[256,1024]{1,0:T(8,128)(2,1)S(1)}, bf16[256,1024]{1,0:T(8,128)(2,1)}, u32[]{:S(2)}) copy-start(bf16[256,1024]{1,0:T(8,128)(2,1)} %param.15) | copy-start | bytes 1572868
  8.0 427.6 %all-reduce.5.cloned.1.call-start = ((), (), s32[]{:S(2)}) async-start(), calls=%async_computation.4 | async-start | bytes 1048576
  304.3 5.6 %copy-start = (f32[448,1024]{1,0:T(8,128)S(1)}, f32[448,1024]{1,0:T(8,128)}, u32[]{:S(2)}) copy-start(f32[448,1024]{1,0:T(8,128)} %get-tuple-element.180) | copy-start | bytes 5505028
  307.9 130.5 %reduce-scatter.3.cloned.1.call-start = ((), (), s32[]{:S(2)}) async-start(), calls=%async_computation.2 | async-start | bytes 589824 | tf_op jit(solution)/shard_map/reduce_scatter | solution.py:120
  309.8 128.8 %reduce-scatter.5.cloned.1.call-start = ((), (), s32[]{:S(2)}) async-start(), calls=%async_computation.3 | async-start | bytes 589824 | tf_op jit(solution)/shard_map/reduce_scatter | solution.py:121
Sparse Core Ops, SparseCore 0:
  308.0 127.5 all-reduce.4
Sparse Core Ops, SparseCore 1:
  312.2 61.1 reduce-scatter.2
  377.6 61.0 reduce-scatter.4
where the time goes:
time: 448 us; the launch traced here: 446 us
  blocking collectives  194 us (43%)
  waiting for transfers between devices  122 us (27%)
  matrix products  64.5 us (14%)
  local copies, waits for them, and re-layouts  34.2 us (8%)
  between operations  16.9 us (4%)
  other arithmetic  13.9 us (3%)
    unnamed x4, waiting for transfers between devices  122 us
    all_gather x1, blocking collectives, on_device(): lax.all_gather(root_keys, ('mid', 'leaf'), axis=0, tiled=True)  65.8 us
    all_gather x1, blocking collectives, on_device(): lax.all_gather(root_values, ('mid', 'leaf'), axis=0, tiled=True)  64.3 us
    all_gather x1, blocking collectives, on_device(): lax.all_gather(mid_keys, 'leaf', axis=0, tiled=True)  32.7 us
    all_gather x1, blocking collectives, on_device(): lax.all_gather(mid_values, 'leaf', axis=0, tiled=True)  31 us
    dot_general x8, matrix products, one_head(): jnp.einsum('gij,igd->jd', probs_low, grad_part, preferred_element_type=jn...  21.9 us
    sub x8, matrix products, one_head(): weights = jnp.exp(scores - row_max)  13.2 us
    dot_general x8, matrix products, one_head(): jnp.einsum('igd,jd->gij', grad_part, value_part, preferred_element_type=j...  10.5 us
  transfers between devices with their start and end apart: 3, of which 2 were waited for; matrix products, arithmetic and copies ran while one was open for 2% of the time, Pallas kernels for 0%

commit v1 on v0

v1 whole, which is shorter than its diff:
```python
import functools
import math

import jax
import jax.numpy as jnp
from jax import lax
from jax.experimental import pallas as pl
from jax.experimental.pallas import tpu as pltpu
from jax.sharding import PartitionSpec as P

HD = 128
FACTOR = HD**-0.5
LOG2E = math.log2(math.e)
CHUNK = 16
NEG = -1e30
NT = (((1,), (1,)), ((), ()))
NN = (((1,), (0,)), ((), ()))
TN = (((0,), (0,)), ((), ()))


def dot(a, b, dims):
    return lax.dot_general(a, b, dims, preferred_element_type=jnp.float32)


def stacked(ref, part, half, heads_per):
    rows = slice(part * half, (part + 1) * half)
    return jnp.concatenate([ref[rows, h * HD : (h + 1) * HD] for h in range(heads_per)], 0)


def fold(x):
    return [x[i : i + 8] for i in range(0, x.shape[0], 8)]


def total_of(so_far, x, op):
    for y in fold(x):
        so_far = y if so_far is None else op(so_far, y)
    return so_far


def own_kernel(
    parity, _, q_hbm, g_hbm, k_hbm, v_hbm, q_ref, g_ref, k_ref, v_ref, e_ref, dp_ref, stats_ref, sems
):
    count, leaf_rows, span = q_ref.shape
    half = leaf_rows // 2
    heads_per = span // HD
    lanes = heads_per * half

    def copies(i):
        h = 2 * i + parity
        wide = pl.ds(pl.multiple_of(h * span, span), span)
        at = pl.ds(pl.multiple_of(h * HD, HD), HD)
        pairs = [
            (q_hbm.at[:, wide], q_ref.at[i]),
            (g_hbm.at[:, wide], g_ref.at[i]),
            (k_hbm.at[:, at], k_ref.at[i]),
            (v_hbm.at[:, at], v_ref.at[i]),
        ]
        return [pltpu.make_async_copy(x, y, sems.at[i, j]) for j, (x, y) in enumerate(pairs)]

    for i in range(count):
        for c in copies(i):
            c.start()
    chunk_row = lax.broadcasted_iota(jnp.int32, (CHUNK, half), 0)
    chunk_col = lax.broadcasted_iota(jnp.int32, (CHUNK, half), 1)

    @pl.loop(0, count)
    def one_head(i):
        for c in copies(i):
            c.wait()

        def scores(part):
            n, at = (part + 1) * half, part * half
            e_ref[i, at : at + n] = dot(k_ref[i, :n], stacked(q_ref.at[i], part, half, heads_per), NT)
            dp_ref[i, at : at + n] = dot(v_ref[i, :n], stacked(g_ref.at[i], part, half, heads_per), NT)

        def softmax(part):
            n, at = (part + 1) * half, part * half
            cols = slice(part * lanes, (part + 1) * lanes)

            def masked_chunk(r):
                s = e_ref[i, at + r : at + r + CHUNK]
                if r < n - half:
                    return s
                mask = chunk_row + (r - n + half) <= chunk_col
                return jnp.concatenate(
                    [jnp.where(mask, s[:, g * half : (g + 1) * half], NEG) for g in range(heads_per)], 1
                )

            starts = range(0, n, CHUNK)
            top = total = rd = None
            for r in starts:
                top = total_of(top, masked_chunk(r), jnp.maximum)
            top = jnp.max(top, axis=0, keepdims=True)
            for r in starts:
                e = jnp.exp2((masked_chunk(r) - top) * (FACTOR * LOG2E))
                e_ref[i, at + r : at + r + CHUNK] = e
                total = total_of(total, e, jnp.add)
                rd = total_of(rd, e * dp_ref[i, at + r : at + r + CHUNK], jnp.add)
            stats_ref[i, 0:1, cols] = top
            stats_ref[i, 1:2, cols] = jnp.sum(total, axis=0, keepdims=True)
            stats_ref[i, 2:3, cols] = jnp.sum(rd, axis=0, keepdims=True)

        scores(0)
        scores(1)
        softmax(0)
        softmax(1)


def places(slots):
    if slots < 4:
        return [(s, 0) for s in range(slots)]
    return [(0, 0), (1, 0), (2, 0), (2, 1)] + [(s - 1, 0) for s in range(4, slots)]


def terms_kernel(slots, mid_part, where_ref, mid_len_ref, leaf_len_ref, *refs):
    own_parts = refs[:7], refs[7:14]
    arrays = places(slots)[-1][0] + 1
    block_refs = [refs[14 + i].at[pl.ds(j * 2 * mid_part, 2 * mid_part)] for i, j in places(slots)]
    root_refs = refs[14 + arrays : 16 + arrays]
    outs = refs[16 + arrays :]
    keys_ref, ds_ref, dk_ref, dv_ref = outs[:4]
    dmid_refs = outs[4 : 4 + slots]
    droot_refs = outs[4 + slots : 6 + slots]
    s_refs, dp_refs, p_refs = (outs[6 + slots + 2 * i : 8 + slots + 2 * i] for i in range(3))
    root_half = root_refs[0].shape[0] // 2
    me = where_ref[0]
    mid_live = mid_len_ref[0]
    leaf_live = leaf_len_ref[0]
    pairs, leaf_rows, span = own_parts[0][0].shape
    half = leaf_rows // 2
    heads_per = span // HD
    mid_rows = slots * mid_part
    root_rows = 2 * root_half
    shared = root_rows + mid_rows
    lanes = heads_per * half
    sizes = [shared + half, shared + 2 * half]
    chunk_row = lax.broadcasted_iota(jnp.int32, (CHUNK, half), 0)
    lane = lax.broadcasted_iota(jnp.int32, (1, half), 1)

    def live(part, x):
        alive = lane + part * half < leaf_live
        return jnp.concatenate(
            [jnp.where(alive, x[:, g * half : (g + 1) * half], 0.0) for g in range(heads_per)], 1
        )

    def masked_chunk(s_ref, r):
        s = s_ref[r : r + CHUNK]
        if r < root_rows:
            return s
        slot, rest = divmod(r - root_rows, mid_part)
        mask = chunk_row < mid_live - rest - jnp.bitwise_xor(me, slot) * mid_part
        return jnp.concatenate(
            [jnp.where(mask, s[:, g * half : (g + 1) * half], NEG) for g in range(heads_per)], 1
        )

    class Head:
        def __init__(self, i, parity):
            self.i = i
            self.h = h = 2 * i + parity
            self.at = pl.ds(pl.multiple_of(h * HD, HD), HD)
            q_ref, g_ref, k_ref, _, self.e_ref, self.own_dp_ref, self.stats_ref = own_parts[parity]
            self.keys = self.whole(0)
            self.values = self.whole(1)
            keys_ref[h, :shared] = self.keys
            keys_ref[h, shared:] = k_ref[i]
            self.qs = [stacked(q_ref.at[i], p, half, heads_per) for p in range(2)]
            self.gs = [stacked(g_ref.at[i], p, half, heads_per) for p in range(2)]
            self.dk, self.dv = [None, None], [None, None]

        def whole(self, which):
            at = self.at
            roots = [r[which * root_half : (which + 1) * root_half, at] for r in root_refs]
            mids = [r[which * mid_part : (which + 1) * mid_part, at] for r in block_refs]
            return jnp.concatenate(roots + mids, 0)

        def scores(self, part):
            s_refs[part][...] = dot(self.keys, self.qs[part], NT)
            dp_refs[part][...] = dot(self.values, self.gs[part], NT)

        def softmax(self, part):
            s_ref, dp_ref, p_ref = s_refs[part], dp_refs[part], p_refs[part]
            cols = slice(part * lanes, (part + 1) * lanes)
            own_top = self.stats_ref[self.i, 0:1, cols]
            top = total = rd = None
            starts = range(0, shared, CHUNK)
            for r in starts:
                top = total_of(top, masked_chunk(s_ref, r), jnp.maximum)
            top = jnp.maximum(jnp.max(top, axis=0, keepdims=True), own_top)
            own = jnp.exp2((own_top - top) * (FACTOR * LOG2E))
            for r in starts:
                e = jnp.exp2((masked_chunk(s_ref, r) - top) * (FACTOR * LOG2E))
                s_ref[r : r + CHUNK] = e
                total = total_of(total, e, jnp.add)
                rd = total_of(rd, e * dp_ref[r : r + CHUNK], jnp.add)
            total = jnp.sum(total, axis=0, keepdims=True) + own * self.stats_ref[self.i, 1:2, cols]
            inv = live(part, 1.0 / total)
            rd = jnp.sum(rd, axis=0, keepdims=True) + own * self.stats_ref[self.i, 2:3, cols]
            rd = rd * inv
            at = part * sizes[0]

            def finish(to, e, dp, scale):
                p = e * scale
                p_ref[to : to + CHUNK] = p.astype(jnp.bfloat16)
                ds_ref[self.h, at + to : at + to + CHUNK] = (p * (dp - rd)).astype(jnp.bfloat16)

            for r in starts:
                finish(r, s_ref[r : r + CHUNK], dp_ref[r : r + CHUNK], inv)
            own = own * inv
            for r in range(0, (part + 1) * half, CHUNK):
                source = slice(part * half + r, part * half + r + CHUNK)
                finish(shared + r, self.e_ref[self.i, source], self.own_dp_ref[self.i, source], own)

        def grads(self, part):
            n = sizes[part]
            at = part * sizes[0]
            self.dv[part] = dot(p_refs[part][:n], self.gs[part], NN)
            self.dk[part] = dot(ds_ref[self.h, at : at + n], self.qs[part], NN)

        def finish(self):
            m = sizes[0]
            dk, dv = (jnp.concatenate([x[0] + x[1][:m], x[1][m:]], 0) for x in (self.dk, self.dv))
            dk = dk * FACTOR
            at = self.at
            dk_ref[:, at] = dk[shared:].astype(jnp.bfloat16)
            dv_ref[:, at] = dv[shared:].astype(jnp.bfloat16)
            for i, o in enumerate(droot_refs):
                r = slice(i * root_half, (i + 1) * root_half)
                o[:, at] = jnp.concatenate([dk[r], dv[r]], 0).astype(jnp.bfloat16)
            for s, o in enumerate(dmid_refs):
                r = slice(root_rows + s * mid_part, root_rows + (s + 1) * mid_part)
                o[:, at] = jnp.concatenate([dk[r], dv[r]], 0).astype(jnp.bfloat16)

    @pl.loop(0, pairs)
    def two_heads(i):
        a, b = Head(i, 0), Head(i, 1)
        a.scores(0)
        a.scores(1)
        a.softmax(0)
        a.grads(0)
        b.scores(0)
        a.softmax(1)
        a.grads(1)
        b.scores(1)
        b.softmax(0)
        a.finish()
        b.grads(0)
        b.softmax(1)
        b.grads(1)
        b.finish()


def query_grads_kernel(heads_per, first, count, half, carried, _, keys_ref, ds_ref, *refs):
    dq_hbm, dq_ref, sems, carried_sems = refs[-4 - carried], *refs[-3:]
    n_all = keys_ref.shape[1]
    span = heads_per * HD
    moves = [
        pltpu.make_async_copy(refs[i], refs[i - 3 - carried], carried_sems.at[i]) for i in range(carried)
    ]
    for c in moves:
        c.start()

    def copy_out(i):
        at = pl.ds(pl.multiple_of(i * span, span), span)
        to = pl.ds(pl.multiple_of((i + first) * span, span), span)
        return pltpu.make_async_copy(dq_ref.at[:, at], dq_hbm.at[:, to], sems.at[i])

    @pl.loop(0, count)
    def one_head(i):
        keys = keys_ref[i + first]
        start = 0
        for part in range(2):
            n = n_all - (1 - part) * half
            dq = dot(keys[:n], ds_ref[i + first, start : start + n], TN)
            dq = (dq * FACTOR).T.astype(jnp.bfloat16)
            start += n
            for g in range(heads_per):
                at = pl.ds(pl.multiple_of(i * span + g * HD, HD), HD)
                dq_ref[part * half : (part + 1) * half, at] = dq[g * half : (g + 1) * half]
        copy_out(i).start()

    for c in moves:
        c.wait()
    for i in range(count):
        copy_out(i).wait()


def cost(matmuls, key_rows, queries, nbytes):
    rows, cols = queries.shape
    return pl.CostEstimate(
        flops=2 * matmuls * rows * key_rows * cols,
        bytes_accessed=nbytes,
        transcendentals=rows * key_rows * cols // HD,
    )


def in_hbm(*arrays):
    return [pltpu.with_memory_space_constraint(x, pltpu.HBM) for x in arrays]


ANY = pl.BlockSpec(memory_space=pl.ANY)
VMEM = pl.BlockSpec(memory_space=pltpu.VMEM)
SMEM = pl.BlockSpec(memory_space=pltpu.SMEM)


def own_part(parity, first, queries, out_grad, leaf_keys, leaf_values):
    rows, cols = leaf_keys.shape
    count = cols // (2 * HD)
    span = queries.shape[1] // cols * HD
    lanes = span // HD * rows // 2
    bf, f32 = jnp.bfloat16, jnp.float32
    shapes = [((rows, span), bf)] * 2 + [((rows, HD), bf)] * 2
    shapes += [((3 * rows // 2, lanes), f32)] * 2 + [((8, 2 * lanes), f32)]
    return pl.pallas_call(
        functools.partial(own_kernel, parity),
        in_specs=[ANY] * 5,
        out_specs=[VMEM] * len(shapes),
        out_shape=[jax.ShapeDtypeStruct((count,) + s, t) for s, t in shapes],
        scratch_shapes=[pltpu.SemaphoreType.DMA((count, 4))],
        compiler_params=pltpu.CompilerParams(vmem_limit_bytes=16 << 20),
        cost_estimate=cost(1, rows, queries, 2 * queries.size),
    )(first, *in_hbm(queries, out_grad, leaf_keys, leaf_values))


def terms_part(where, mid_len, leaf_len, slots, own, blocks, roots, mid_part):
    pairs, leaf_rows, span = own[0][0].shape
    cols = blocks[0].shape[1]
    heads = 2 * pairs
    shared = slots * mid_part + roots[0].shape[0]
    key_rows = shared + leaf_rows
    half = leaf_rows // 2
    lanes = span // HD * half
    bf, f32 = jnp.bfloat16, jnp.float32
    shapes = [
        (heads, key_rows, HD),
        (heads, 2 * key_rows - half, lanes),
        (leaf_rows, cols),
        (leaf_rows, cols),
    ]
    shapes += [(2 * mid_part, cols)] * slots + [x.shape for x in roots]
    out = pl.pallas_call(
        functools.partial(terms_kernel, slots, mid_part),
        in_specs=[SMEM] * 3 + [VMEM] * (16 + len(blocks)),
        out_specs=[VMEM] * len(shapes),
        out_shape=[jax.ShapeDtypeStruct(s, bf) for s in shapes],
        scratch_shapes=[pltpu.VMEM((shared, lanes), f32) for _ in range(4)]
        + [pltpu.VMEM((key_rows, lanes), bf) for _ in range(2)],
        compiler_params=pltpu.CompilerParams(vmem_limit_bytes=(14 if shared <= 256 else 40) << 20),
        cost_estimate=pl.CostEstimate(
            flops=8 * leaf_rows * key_rows * span * heads,
            bytes_accessed=4 * leaf_rows * span * heads,
            transcendentals=leaf_rows * key_rows * heads,
        ),
    )(where, mid_len, leaf_len, *own[0], *own[1], *blocks, *roots)
    return out[0], out[1], out[2:4], out[4 : 4 + slots], out[4 + slots :]


def query_grads(after_this, first, count, so_far, queries, keys, ds, carried=()):
    rows, cols = queries.shape
    heads = keys.shape[0]
    heads_per = cols // (heads * HD)
    like = [jax.ShapeDtypeStruct(x.shape, x.dtype) for x in (queries, *carried)]
    return pl.pallas_call(
        functools.partial(query_grads_kernel, heads_per, first, count, rows // 2, len(carried)),
        in_specs=[ANY] + [VMEM] * (2 + len(carried)) + [ANY] * len(so_far),
        out_specs=[ANY] * len(like),
        out_shape=like,
        input_output_aliases={3 + len(carried) + i: i for i in range(len(so_far))},
        scratch_shapes=[
            pltpu.VMEM((rows, count * heads_per * HD), jnp.bfloat16),
            pltpu.SemaphoreType.DMA((count,)),
            pltpu.SemaphoreType.DMA((max(len(carried), 1),)),
        ],
        compiler_params=pltpu.CompilerParams(
            vmem_limit_bytes=(10 if keys.shape[1] <= 512 else 32) << 20
        ),
        cost_estimate=cost(1, keys.shape[1] * count // heads, queries, 2 * queries.size),
    )(after_this, keys, ds, *carried, *so_far)


def gather_kernel(mk_ref, mv_ref, rk_ref, rv_ref, mid_ref, pair_ref):
    mid_ref[...] = jnp.concatenate([mk_ref[...], mv_ref[...]], 0)
    pair_ref[...] = jnp.concatenate([rk_ref[...], rv_ref[...]], 0)


def gather_own(mid_keys, mid_values, root_keys, root_values):
    return pl.pallas_call(
        gather_kernel,
        out_shape=[
            jax.ShapeDtypeStruct((2 * x.shape[0], x.shape[1]), x.dtype)
            for x in (mid_keys, root_keys)
        ],
        compiler_params=pltpu.CompilerParams(vmem_limit_bytes=4 << 20),
    )(*in_hbm(mid_keys, mid_values, root_keys, root_values))


def pack_kernel(root_own, where_ref, mid_len_ref, leaf_len_ref, mid_ref, *refs):
    pairs = [r[...].astype(jnp.float32) for r in refs[:-1]]
    roots = [p[:root_own] for p in pairs] + [p[root_own:] for p in pairs]
    refs[-1][...] = jnp.concatenate(
        [mid_ref[...], jnp.concatenate(roots, 0).astype(jnp.bfloat16)], 0
    )


def pack(scalars, mid, pairs):
    rows = mid.shape[0] + len(pairs) * pairs[0].shape[0]
    return pl.pallas_call(
        functools.partial(pack_kernel, pairs[0].shape[0] // 2),
        in_specs=[SMEM] * 3 + [VMEM] * (1 + len(pairs)),
        out_shape=jax.ShapeDtypeStruct((rows, mid.shape[1]), jnp.bfloat16),
        compiler_params=pltpu.CompilerParams(vmem_limit_bytes=4 << 20),
    )(*scalars, mid, *pairs)


def join_kernel(mid_rows, _, a_ref, b_ref, out_ref):
    rows = a_ref.shape[0]
    out_ref[:mid_rows] = a_ref[:mid_rows]
    out_ref[mid_rows : 2 * mid_rows] = b_ref[:mid_rows]
    roots = [r[mid_rows:rows].astype(jnp.float32) for r in (a_ref, b_ref)]
    out_ref[2 * mid_rows :] = jnp.concatenate(roots, 0).astype(jnp.bfloat16)


def join(first, a, b, mid_rows):
    return pl.pallas_call(
        functools.partial(join_kernel, mid_rows),
        out_shape=jax.ShapeDtypeStruct((2 * a.shape[0], a.shape[1]), a.dtype),
        compiler_params=pltpu.CompilerParams(vmem_limit_bytes=4 << 20),
    )(first, a, b)


def root_of(ref, mid_rows, place):
    if place is None:
        return ref[mid_rows:].astype(jnp.float32)
    both = ref[2 * mid_rows :].astype(jnp.float32)
    rows = both.shape[0] // 2
    return both[place * rows : (place + 1) * rows]


def two_level(slots):
    found = places(slots)
    return [(i, j if slots >= 4 and i == 2 else None) for i, j in found]


def collect_kernel(slots, mid_rows, _, *refs):
    out_ref = refs[-1]
    roots = [root_of(refs[i], mid_rows, j) for i, j in two_level(slots)]
    half = roots[0].shape[0] // 2
    out_ref[...] = jnp.concatenate(
        [r[:half] for r in roots] + [r[half:] for r in roots], 0
    ).astype(jnp.bfloat16)


def collect(first, blocks, slots, mid_rows):
    rows = slots * (blocks[0].shape[0] - mid_rows)
    return pl.pallas_call(
        functools.partial(collect_kernel, slots, mid_rows),
        in_specs=[ANY] + [VMEM] * len(blocks),
        out_shape=jax.ShapeDtypeStruct((rows, blocks[0].shape[1]), jnp.bfloat16),
        compiler_params=pltpu.CompilerParams(vmem_limit_bytes=8 << 20),
    )(first, *blocks)


def spread_kernel(slots, mid_rows, a_ref, b_ref, *refs):
    mids, outs = refs[:slots], refs[slots:]
    total = a_ref[...].astype(jnp.float32) + b_ref[...].astype(jnp.float32)
    half = total.shape[0] // 2
    part = half // slots
    roots = [
        jnp.concatenate([total[at + s * part : at + (s + 1) * part] for at in (0, half)], 0)
        for s in range(slots)
    ]
    held = {}
    for s, (i, j) in enumerate(two_level(slots)):
        at = mid_rows * (j or 0)
        outs[i][at : at + mid_rows] = mids[s][...]
        held.setdefault(i, []).append(roots[s])
    for i, x in held.items():
        outs[i][len(x) * mid_rows :] = jnp.concatenate(x, 0).astype(jnp.bfloat16)


def spread(a, b, mids):
    slots = len(mids)
    mid_rows, cols = mids[0].shape
    rows = mid_rows + a.shape[0] // slots
    arrays = places(slots)[-1][0] + 1
    shapes = [(2 * rows if slots >= 4 and i == 2 else rows, cols) for i in range(arrays)]
    return pl.pallas_call(
        functools.partial(spread_kernel, slots, mid_rows),
        out_shape=[jax.ShapeDtypeStruct(x, jnp.bfloat16) for x in shapes],
        compiler_params=pltpu.CompilerParams(vmem_limit_bytes=8 << 20),
    )(a, b, *mids)


def near_sum_kernel(mid_rows, a_ref, pair_ref, out_ref):
    pair = pair_ref[mid_rows : 2 * mid_rows].astype(jnp.float32)
    out_ref[:mid_rows] = (a_ref[:mid_rows].astype(jnp.float32) + pair).astype(jnp.bfloat16)
    root = root_of(a_ref, mid_rows, None) + root_of(pair_ref, mid_rows, 1)
    out_ref[mid_rows:] = root.astype(jnp.bfloat16)


def near_sum(a, pair, mid_rows):
    return pl.pallas_call(
        functools.partial(near_sum_kernel, mid_rows),
        out_shape=jax.ShapeDtypeStruct(a.shape, a.dtype),
        compiler_params=pltpu.CompilerParams(vmem_limit_bytes=4 << 20),
    )(a, pair)


def far_sum_kernel(_, a_ref, b_ref, out_ref):
    out_ref[...] = (a_ref[...].astype(jnp.float32) + b_ref[...].astype(jnp.float32)).astype(jnp.bfloat16)


def far_sum(first, a, b):
    return pl.pallas_call(
        far_sum_kernel,
        in_specs=[ANY] + [VMEM] * 2,
        out_shape=jax.ShapeDtypeStruct(a.shape, a.dtype),
        compiler_params=pltpu.CompilerParams(vmem_limit_bytes=4 << 20),
    )(first, a, b)


def after_kernel(*refs):
    pass


def after(first, arrays):
    return pl.pallas_call(
        after_kernel,
        in_specs=[VMEM] + [ANY] * len(arrays),
        out_specs=[ANY] * len(arrays),
        out_shape=[jax.ShapeDtypeStruct(x.shape, x.dtype) for x in arrays],
        input_output_aliases={1 + i: i for i in range(len(arrays))},
        compiler_params=pltpu.CompilerParams(vmem_limit_bytes=4 << 20),
    )(first, *arrays)


def mid_sums_kernel(mid_part, *refs):
    for i, o in enumerate(refs[-2:]):
        rows = slice(i * mid_part, (i + 1) * mid_part)
        total = refs[0][rows].astype(jnp.float32)
        for r in refs[1:-2]:
            total = total + r[rows].astype(jnp.float32)
        o[...] = total


def mid_sums(blocks, mid_part):
    return pl.pallas_call(
        functools.partial(mid_sums_kernel, mid_part),
        out_shape=[jax.ShapeDtypeStruct((mid_part, blocks[0].shape[1]), jnp.float32)] * 2,
        compiler_params=pltpu.CompilerParams(vmem_limit_bytes=8 << 20),
    )(*blocks)


def root_sums_kernel(count, mid_rows, root_own, paired, _, *refs):
    root = None
    for i, r in enumerate(refs[:count]):
        x = root_of(r, mid_rows, 0 if paired and i == 1 else None)
        root = x if root is None else root + x
    half = root.shape[0] // 2
    for t, o in enumerate(refs[count:]):
        o[:root_own] = root[t * root_own : (t + 1) * root_own]
        o[root_own:] = root[half + t * root_own : half + (t + 1) * root_own]


def root_sums(first, blocks, mid_rows, root_own, pieces):
    shape = jax.ShapeDtypeStruct((2 * root_own, blocks[0].shape[1]), jnp.float32)
    paired = blocks[1].shape[0] > blocks[0].shape[0]
    return pl.pallas_call(
        functools.partial(root_sums_kernel, len(blocks), mid_rows, root_own, paired),
        in_specs=[ANY] + [VMEM] * len(blocks),
        out_shape=[shape] * pieces,
        compiler_params=pltpu.CompilerParams(vmem_limit_bytes=8 << 20),
    )(*in_hbm(first), *blocks)


def root_kernel(root_own, *refs):
    total = refs[0][...]
    for r in refs[1:-2]:
        total = total + r[...]
    refs[-2][...] = total[:root_own]
    refs[-1][...] = total[root_own:]


def add_roots(pieces):
    rows, cols = pieces[0].shape
    return pl.pallas_call(
        functools.partial(root_kernel, rows // 2),
        out_shape=[jax.ShapeDtypeStruct((rows // 2, cols), jnp.float32)] * 2,
        compiler_params=pltpu.CompilerParams(vmem_limit_bytes=4 << 20),
    )(*pieces)


def swap(x, axis, size, offset):
    return lax.ppermute(x, axis, [(i, i ^ offset) for i in range(size)])


def on_device(
    mids,
    leaves,
    queries,
    out_grad,
    leaf_keys,
    leaf_values,
    mid_keys,
    mid_values,
    root_keys,
    root_values,
    mid_len,
    leaf_len,
):
    mid_part = mid_keys.shape[0]
    root_own = root_keys.shape[0]
    where = lax.axis_index("leaf").reshape(1).astype(jnp.int32)
    mid, pair = gather_own(mid_keys, mid_values, root_keys, root_values)
    mid_rows = 2 * mid_part
    same_core = range(2, mids, 2)
    pairs = [pair] + [swap(pair, "mid", mids, t) for t in same_core]
    block = pack((where, mid_len, leaf_len), mid, pairs)

    def leaf_swap(x, s):
        return swap(x, "leaf", leaves, s)

    far = list(reversed(range(4, leaves, 2)))
    far_blocks = [leaf_swap(block, s) for s in far]
    beside = leaf_swap(block, 1)
    operands = (queries, out_grad, leaf_keys, leaf_values)
    own = [own_part(0, block, *operands)]
    token = own[0][-1]
    near = leaf_swap(join(token, block, beside, mid_rows), 2)
    far_blocks = after(token, far_blocks)
    own.append(own_part(1, far_blocks[-1] if far else token, *operands))
    blocks = [block, beside, near]
    for x in reversed(far_blocks):
        blocks += [x, leaf_swap(x, 1)]
    root = collect(own[1][-1], blocks, leaves, mid_rows)
    roots = [root, swap(root, "mid", mids, 1)]
    keys, ds, leaf_grads, mid_terms, root_terms = terms_part(
        where, mid_len, leaf_len, leaves, own, blocks, roots, mid_part
    )

    terms = spread(root_terms[0], swap(root_terms[1], "mid", mids, 1), mid_terms)
    through = [leaf_swap(terms[s], 1) for s in far]
    near = leaf_swap(terms[2], 2)
    heads = leaf_keys.shape[1] // HD
    early = heads // 2
    query_grad, *leaf_grads = query_grads(terms[0], 0, early, (), queries, keys, ds, leaf_grads)
    leaf_key_grad, leaf_value_grad = leaf_grads
    token = in_hbm(leaf_value_grad)[0]
    arrived = [terms[0], near]
    for s, x in zip(far, through):
        arrived.append(leaf_swap(far_sum(token, terms[s - 1], x), s))
    arrived.append(leaf_swap(near_sum(terms[1], near, mid_rows), 1))
    (query_grad,) = query_grads(terms[0], early, heads - early, (query_grad,), queries, keys, ds)
    pieces = root_sums(query_grad, arrived, mid_rows, root_own, mids // 2)
    mid_key_grad, mid_value_grad = mid_sums(arrived, mid_part)
    pieces = [pieces[0]] + [swap(x, "mid", mids, t) for t, x in zip(same_core, pieces[1:])]
    root_key_grad, root_value_grad = add_roots(pieces)
    return (
        query_grad,
        leaf_key_grad,
        leaf_value_grad,
        mid_key_grad,
        mid_value_grad,
        root_key_grad,
        root_value_grad,
    )


def solution(mesh):
    both = P(("mid", "leaf"), None)
    in_specs = (both,) * 8 + (P("mid"), P(("mid", "leaf")))
    return jax.shard_map(
        functools.partial(on_device, mesh.shape["mid"], mesh.shape["leaf"]),
        mesh=mesh,
        in_specs=in_specs,
        out_specs=(both,) * 7,
        check_vma=False,
    )
```

time: 448 us -> 53.7 us (0.12)
  blocking collectives: 194 us -> 0 us
  waiting for transfers between devices: 122 us -> 9.42 us
  matrix products: 64.5 us -> 0 us
  local copies, waits for them, and re-layouts: 34.2 us -> 0 us
  Pallas kernels: 0 us -> 21.3 us
  starting transfers between devices: 0.13 us -> 20.7 us
  between operations: 16.9 us -> 2.07 us
  other arithmetic: 13.9 us -> 0 us
    all_gather x4 -> x0, blocking collectives: 194 us -> none  [the longest x1 65.8 us: on_device(): lax.all_gather(root_keys, ('mid', 'leaf'), axis=0, tiled=True)]
    unnamed x4 -> x0, waiting for transfers between devices: 122 us -> none
    dot_general x32 -> x0, matrix products: 51.3 us -> none  [the longest x8 21.9 us: one_head(): jnp.einsum('gij,igd->jd', probs_low, grad_part, preferred_element_type=jn...]
    pallas_call x0 -> x17, Pallas kernels: none -> 21.3 us  [the longest x1 7.87 us: terms_part(): pl.pallas_call(functools.partial(terms_kernel, slots, mid_part), in_specs...]
    ppermute x0 -> x16, starting transfers between devices: none -> 20.7 us  [swap(): return lax.ppermute(x, axis, [(i, i ^ offset) for i in range(size)])]
    sub x8 -> x0, matrix products: 13.2 us -> none  [one_head(): weights = jnp.exp(scores - row_max)]
    dynamic_slice x24 -> x0, local copies, waits for them, and re-layouts: 10.7 us -> none  [the longest x16 9.61 us: one_head(): lax.dynamic_slice_in_dim(out_grad, head_index * span_cols, span_cols, 1)]
    ppermute x0 -> x16, waiting for transfers between devices: none -> 9.42 us  [swap(): return lax.ppermute(x, axis, [(i, i ^ offset) for i in range(size)])]
  transfers between devices with their start and end apart: 3 -> 16, of which waited for: 2 -> 9; matrix products, arithmetic and copies ran while one was open for 2% -> 0% of each run, Pallas kernels for 0% -> 22%
where the time goes in v1:
time: 53.7 us; the launch traced here: 53.4 us
  Pallas kernels  21.3 us (40%)
  starting transfers between devices  20.7 us (39%)
  waiting for transfers between devices  9.42 us (18%)
  between operations  2.07 us (4%)
    ppermute x16, starting transfers between devices, swap(): return lax.ppermute(x, axis, [(i, i ^ offset) for i in range(size)])  20.7 us
    ppermute x16, waiting for transfers between devices, swap(): return lax.ppermute(x, axis, [(i, i ^ offset) for i in range(size)])  9.42 us
    pallas_call x1, Pallas kernels, terms_part(): pl.pallas_call(functools.partial(terms_kernel, slots, mid_part), in_specs...  7.87 us
    pallas_call x2, Pallas kernels, own_part(): pl.pallas_call(functools.partial(own_kernel, parity), in_specs=[ANY] * 5,...  6.28 us
    pallas_call x2, Pallas kernels, query_grads(): pl.pallas_call(functools.partial(query_grads_kernel, heads_per, first, co...  4.8 us
  transfers between devices with their start and end apart: 16, of which 9 were waited for; matrix products, arithmetic and copies ran while one was open for 0% of the time, Pallas kernels for 22%

profile of v1, /device:TPU:0, one launch (start us, length us, event | category | flops | bytes accessed | tf_op | source)
XLA Modules:
  0.0 53.4 jit_solution(13644123108369409721)
XLA Ops:
  0.6 0.8 %shard_map.153 = (bf16[32,1024]{1,0:T(8,128)(2,1)S(1)}, bf16[4,1024]{1,0:T(4,128)(2,1)S(1)}) custom-call(bf16[16,1024]{1,0:T(8,128)(2,1)} %mk_ref.1, bf16[16,1024]{1,0:T(8,128)(2,1)} %mv_ref.1, bf16[2,1024]{1,0:T(2,128)(2,1)} %rk_ref.1, bf16[2,1024]{1,0:T(2,128)(2,1)} %rv_ref.1), custom_call_target="tpu_custom_call" | custom-call | tf_op jit(solution)/shard_map/pallas_call | solution.py:386
  1.4 3.0 %collective-permute-start = (bf16[4,1024]{1,0:T(4,128)(2,1)S(1)}, bf16[4,1024]{1,0:T(4,128)(2,1)S(1)}, u32[]{:S(2)}, u32[]{:S(2)}) collective-permute-start(bf16[4,1024]{1,0:T(4,128)(2,1)S(1)} %get-tuple-element.56.refs_0_), channel_id=1, source_target_pairs={{0,16},{8,24},{16,0},{24,8},{1,17},{9,25},{17,1},{25,9},{2,18},{10... | collective-permute-start | bytes 24584 | tf_op jit(solution)/shard_map/ppermute | solution.py:593
  5.8 0.3 collective-permute-done.refs_1_
  6.1 2.1 %collective-permute-start.3 = (bf16[40,1024]{1,0:T(8,128)(2,1)S(1)}, bf16[40,1024]{1,0:T(8,128)(2,1)S(1)}, u32[]{:S(2)}, u32[]{:S(2)}) collective-permute-start(bf16[40,1024]{1,0:T(8,128)(2,1)S(1)} %shard_map.154._.a_ref.refs_0_.refs_14_), channel_id=1, source_target_pairs={{0,1},{1,0},{2,3},{3,2},{4,5},{5,4},{6,7},{7,6},{8,9},{9,8},{10,11... | collective-permute-start | bytes 245768 | tf_op jit(solution)/shard_map/ppermute | solution.py:593
  8.2 2.6 %collective-permute-start.2 = (bf16[40,1024]{1,0:T(8,128)(2,1)S(1)}, bf16[40,1024]{1,0:T(8,128)(2,1)S(1)}, u32[]{:S(2)}, u32[]{:S(2)}) collective-permute-start(bf16[40,1024]{1,0:T(8,128)(2,1)S(1)} %shard_map.154._.a_ref.refs_0_.refs_14_), channel_id=1, source_target_pairs={{0,4},{1,5},{2,6},{3,7},{4,0},{5,1},{6,2},{7,3},{8,12},{9,13},{10,... | collective-permute-start | bytes 245768 | tf_op jit(solution)/shard_map/ppermute | solution.py:593
  10.8 1.3 %collective-permute-start.1 = (bf16[40,1024]{1,0:T(8,128)(2,1)S(1)}, bf16[40,1024]{1,0:T(8,128)(2,1)S(1)}, u32[]{:S(2)}, u32[]{:S(2)}) collective-permute-start(bf16[40,1024]{1,0:T(8,128)(2,1)S(1)} %shard_map.154._.a_ref.refs_0_.refs_14_), channel_id=1, source_target_pairs={{0,6},{1,7},{2,4},{3,5},{4,2},{5,3},{6,0},{7,1},{8,14},{9,15},{10,... | collective-permute-start | bytes 245768 | tf_op jit(solution)/shard_map/ppermute | solution.py:593
  12.1 3.1 %shard_map.155 = (bf16[4,256,512]{2,1,0:T(8,128)(2,1)S(1)}, bf16[4,256,512]{2,1,0:T(8,128)(2,1)S(1)}, bf16[4,256,128]{2,1,0:T(8,128)(2,1)S(1)}, bf16[4,256,128]{...) custom-call(bf16[40,1024]{1,0:T(8,128)(2,1)S(1)} %shard_map.154._.a_ref.r, ...), custom_call_target="tpu_custom_call" | custom-call | flops 536870912 | bytes 2097152 | tf_op jit(solution)/shard_map/pallas_call | solution.py:313
  15.3 0.3 collective-permute-start.4
  15.6 0.6 %collective-permute-done.2.refs_2_ = bf16[40,1024]{1,0:T(8,128)(2,1)S(1)} collective-permute-done((bf16[40,1024]{1,0:T(8,128)(2,1)S(1)}, bf16[40,1024]{1,0:T(8,128)(2,1)S(1)}, u32[]{:S(2)}, u32[]{:S(2)}) %collective-permute-start.2) | collective-permute-done | bytes 81952 | tf_op jit(solution)/shard_map/ppermute | solution.py:593
  16.2 1.0 %collective-permute-done.1.refs_1_ = bf16[40,1024]{1,0:T(8,128)(2,1)S(1)} collective-permute-done((bf16[40,1024]{1,0:T(8,128)(2,1)S(1)}, bf16[40,1024]{1,0:T(8,128)(2,1)S(1)}, u32[]{:S(2)}, u32[]{:S(2)}) %collective-permute-start.1) | collective-permute-done | bytes 81952 | tf_op jit(solution)/shard_map/ppermute | solution.py:593
  17.2 0.5 collective-permute-start.6
  17.7 1.5 %collective-permute-start.5 = (bf16[40,1024]{1,0:T(8,128)(2,1)S(1)}, bf16[40,1024]{1,0:T(8,128)(2,1)S(1)}, u32[]{:S(2)}, u32[]{:S(2)}) collective-permute-start(bf16[40,1024]{1,0:T(8,128)(2,1)S(1)} %get-tuple-element.64._.refs_3_.refs_17_), channel_id=1, source_target_pairs={{0,1},{1,0},{2,3},{3,2},{4,5},{5,4},{6,7},{7,6},{8,9},{9,8},{10,11... | collective-permute-start | bytes 245768 | tf_op jit(solution)/shard_map/ppermute | solution.py:593
  19.2 3.2 %shard_map.157 = (bf16[4,256,512]{2,1,0:T(8,128)(2,1)S(1)}, bf16[4,256,512]{2,1,0:T(8,128)(2,1)S(1)}, bf16[4,256,128]{2,1,0:T(8,128)(2,1)S(1)}, bf16[4,256,128]{...) custom-call(bf16[40,1024]{1,0:T(8,128)(2,1)S(1)} %get-tuple-element.64._., ...), custom_call_target="tpu_custom_call" | custom-call | flops 536870912 | bytes 2097152 | tf_op jit(solution)/shard_map/pallas_call | solution.py:313
  22.4 0.1 collective-permute-done.5.refs_4_.refs_18_
  22.6 1.3 %collective-permute-done.7.refs_22_ = bf16[64,1024]{1,0:T(8,128)(2,1)S(1)} collective-permute-done((bf16[64,1024]{1,0:T(8,128)(2,1)S(1)}, bf16[64,1024]{1,0:T(8,128)(2,1)S(1)}, u32[]{:S(2)}, u32[]{:S(2)}) %collective-permute-start.7) | collective-permute-done | bytes 131104 | tf_op jit(solution)/shard_map/ppermute | solution.py:593
  23.9 7.9 %shard_map.160 = (bf16[8,448,128]{2,1,0:T(8,128)(2,1)S(1)}, bf16[8,768,512]{2,1,0:T(8,128)(2,1)S(1)}, bf16[256,1024]{1,0:T(8,128)(2,1)S(1)}, bf16[256,1024]{1,0:...) custom-call(s32[1]{0:T(128)} %bitcast.where_ref, ...), custom_call_target="tpu_custom_call" | custom-call | flops 3758096384 | bytes 4194304 | tf_op jit(solution)/shard_map/pallas_call | solution.py:340
  31.8 0.2 collective-permute-start.8
  32.0 1.2 %collective-permute-done.8.b_ref = bf16[64,1024]{1,0:T(8,128)(2,1)S(1)} collective-permute-done((bf16[64,1024]{1,0:T(8,128)(2,1)S(1)}, bf16[64,1024]{1,0:T(8,128)(2,1)S(1)}, u32[]{:S(2)}, u32[]{:S(2)}) %collective-permute-start.8) | collective-permute-done | bytes 131104 | tf_op jit(solution)/shard_map/ppermute | solution.py:593
  33.2 0.1 shard_map.161
  33.3 1.3 %collective-permute-start.9 = (bf16[80,1024]{1,0:T(8,128)(2,1)S(1)}, bf16[80,1024]{1,0:T(8,128)(2,1)S(1)}, u32[]{:S(2)}, u32[]{:S(2)}) collective-permute-start(bf16[80,1024]{1,0:T(8,128)(2,1)S(1)} %get-tuple-element.91), channel_id=1, source_target_pairs={{0,2},{1,3},{2,0},{3,1},{4,6},{5,7},{6,4},{7,5},{8,10},{9,11},{10,... | collective-permute-start | bytes 491528 | tf_op jit(solution)/shard_map/ppermute | solution.py:593
  34.6 1.2 %collective-permute-start.10 = (bf16[40,1024]{1,0:T(8,128)(2,1)S(1)}, bf16[40,1024]{1,0:T(8,128)(2,1)S(1)}, u32[]{:S(2)}, u32[]{:S(2)}) collective-permute-start(bf16[40,1024]{1,0:T(8,128)(2,1)S(1)} %get-tuple-element.93), channel_id=1, source_target_pairs={{0,1},{1,0},{2,3},{3,2},{4,5},{5,4},{6,7},{7,6},{8,9},{9,8},{10,11... | collective-permute-start | bytes 245768 | tf_op jit(solution)/shard_map/ppermute | solution.py:593
  35.7 0.9 %collective-permute-start.12 = (bf16[40,1024]{1,0:T(8,128)(2,1)S(1)}, bf16[40,1024]{1,0:T(8,128)(2,1)S(1)}, u32[]{:S(2)}, u32[]{:S(2)}) collective-permute-start(bf16[40,1024]{1,0:T(8,128)(2,1)S(1)} %get-tuple-element.95), channel_id=1, source_target_pairs={{0,1},{1,0},{2,3},{3,2},{4,5},{5,4},{6,7},{7,6},{8,9},{9,8},{10,11... | collective-permute-start | bytes 245768 | tf_op jit(solution)/shard_map/ppermute | solution.py:593
  36.6 2.4 %shard_map.162 = (bf16[256,4096]{1,0:T(8,128)(2,1)}, bf16[256,1024]{1,0:T(8,128)(2,1)}, bf16[256,1024]{1,0:T(8,128)(2,1)}) custom-call(bf16[40,1024]{1,0:T(8,128)(2,1)S(1)} %get-tuple-element.83._.refs_0_, bf16[8,448,128]{2,1,0:T(8,128)(2,1)S(1)} %get-tuple-element.84.keys_ref, bf16[8,768,512]{2,1,0:T(8,128)(2,1)S(1)} %get-tuple-element.85.ds_ref, ...), custom_call_target="tpu_custom_call" | custom-call | flops 469762048 | bytes 2097152 | tf_op jit(solution)/shard_map/pallas_call | solution.py:362
  39.0 0.7 %collective-permute-done.10.b_ref = bf16[40,1024]{1,0:T(8,128)(2,1)S(1)} collective-permute-done((bf16[40,1024]{1,0:T(8,128)(2,1)S(1)}, bf16[40,1024]{1,0:T(8,128)(2,1)S(1)}, u32[]{:S(2)}, u32[]{:S(2)}) %collective-permute-start.10) | collective-permute-done | bytes 81952 | tf_op jit(solution)/shard_map/ppermute | solution.py:593
  39.7 2.9 %collective-permute-start.11 = (bf16[40,1024]{1,0:T(8,128)(2,1)S(1)}, bf16[40,1024]{1,0:T(8,128)(2,1)S(1)}, u32[]{:S(2)}, u32[]{:S(2)}) collective-permute-start(bf16[40,1024]{1,0:T(8,128)(2,1)S(1)} %shard_map.164), channel_id=1, source_target_pairs={{0,6},{1,7},{2,4},{3,5},{4,2},{5,3},{6,0},{7,1},{8,14},{9,15},{10,... | collective-permute-start | bytes 245768 | tf_op jit(solution)/shard_map/ppermute | solution.py:593
  42.8 1.2 %collective-permute-start.14 = (bf16[40,1024]{1,0:T(8,128)(2,1)S(1)}, bf16[40,1024]{1,0:T(8,128)(2,1)S(1)}, u32[]{:S(2)}, u32[]{:S(2)}) collective-permute-start(bf16[40,1024]{1,0:T(8,128)(2,1)S(1)} %shard_map.166), channel_id=1, source_target_pairs={{0,1},{1,0},{2,3},{3,2},{4,5},{5,4},{6,7},{7,6},{8,9},{9,8},{10,11... | collective-permute-start | bytes 245768 | tf_op jit(solution)/shard_map/ppermute | solution.py:593
  44.0 2.4 %shard_map.163._ = bf16[256,4096]{1,0:T(8,128)(2,1)} custom-call(bf16[40,1024]{1,0:T(8,128)(2,1)S(1)} %get-tuple-element.83._.refs_0_, bf16[8,448,128]{2,1,0:T(8,128)(2,1)S(1)} %get-tuple-element.84.keys_ref, bf16[8,768,512]{2,1,0:T(8,128)(2,1)S(1)} %get-tuple-element.85.ds_ref, ...), custom_call_target="tpu_custom_call", output_to_operand_aliasing={{}: (3, {})} | custom-call | flops 469762048 | bytes 2097152 | tf_op jit(solution)/shard_map/pallas_call | solution.py:362
  46.4 2.6 %collective-permute-done.13.refs_3_ = bf16[40,1024]{1,0:T(8,128)(2,1)S(1)} collective-permute-done((bf16[40,1024]{1,0:T(8,128)(2,1)S(1)}, bf16[40,1024]{1,0:T(8,128)(2,1)S(1)}, u32[]{:S(2)}, u32[]{:S(2)}) %collective-permute-start.13) | collective-permute-done | bytes 81952 | tf_op jit(solution)/shard_map/ppermute | solution.py:593
  49.0 1.5 %collective-permute-start.15 = (f32[4,1024]{1,0:T(4,128)S(1)}, f32[4,1024]{1,0:T(4,128)S(1)}, u32[]{:S(2)}, u32[]{:S(2)}) collective-permute-start(f32[4,1024]{1,0:T(4,128)S(1)} %get-tuple-element.100), channel_id=1, source_target_pairs={{0,16},{8,24},{16,0},{24,8},{1,17},{9,25},{17,1},{25,9},{2,18},{10... | collective-permute-start | bytes 49160 | tf_op jit(solution)/shard_map/ppermute | solution.py:593
  50.5 0.7 %shard_map.167 = (f32[16,1024]{1,0:T(8,128)}, f32[16,1024]{1,0:T(8,128)}) custom-call(bf16[40,1024]{1,0:T(8,128)(2,1)S(1)} %get-tuple-element.83._.refs_0_, bf16[80,1024]{1,0:T(8,128)(2,1)S(1)} %collective-permute-done.9.pair_ref.refs_1_, bf16[40,1024]{1,0:T(8,128)(2,1)S(1)} %collective-permute-done.11.refs_2_, ...), custom_call_target="tpu_custom_call" | custom-call | tf_op jit(solution)/shard_map/pallas_call | solution.py:546
  51.2 1.6 %collective-permute-done.15.refs_1_ = f32[4,1024]{1,0:T(4,128)S(1)} collective-permute-done((f32[4,1024]{1,0:T(4,128)S(1)}, f32[4,1024]{1,0:T(4,128)S(1)}, u32[]{:S(2)}, u32[]{:S(2)}) %collective-permute-start.15) | collective-permute-done | bytes 16416 | tf_op jit(solution)/shard_map/ppermute | solution.py:593
  52.8 0.6 %shard_map.169 = (f32[2,1024]{1,0:T(2,128)}, f32[2,1024]{1,0:T(2,128)}) custom-call(f32[4,1024]{1,0:T(4,128)S(1)} %get-tuple-element.99.refs_0_, f32[4,1024]{1,0:T(4,128)S(1)} %collective-permute-done.15.refs_1_), custom_call_target="tpu_custom_call" | custom-call | tf_op jit(solution)/shard_map/pallas_call | solution.py:585
  (17 shorter events, 0.3 us)
Async XLA Ops:
  1.4 4.7 %collective-permute-start = (bf16[4,1024]{1,0:T(4,128)(2,1)S(1)}, bf16[4,1024]{1,0:T(4,128)(2,1)S(1)}, u32[]{:S(2)}, u32[]{:S(2)}) collective-permute-start(bf16[4,1024]{1,0:T(4,128)(2,1)S(1)} %get-tuple-element.56.refs_0_), channel_id=1, source_target_pairs={{0,16},{8,24},{16,0},{24,8},{1,17},{9,25},{17,1},{25,9},{2,18},{10... | collective-permute-start | bytes 24584 | tf_op jit(solution)/shard_map/ppermute | solution.py:593
  6.1 9.1 %collective-permute-start.3 = (bf16[40,1024]{1,0:T(8,128)(2,1)S(1)}, bf16[40,1024]{1,0:T(8,128)(2,1)S(1)}, u32[]{:S(2)}, u32[]{:S(2)}) collective-permute-start(bf16[40,1024]{1,0:T(8,128)(2,1)S(1)} %shard_map.154._.a_ref.refs_0_.refs_14_), channel_id=1, source_target_pairs={{0,1},{1,0},{2,3},{3,2},{4,5},{5,4},{6,7},{7,6},{8,9},{9,8},{10,11... | collective-permute-start | bytes 245768 | tf_op jit(solution)/shard_map/ppermute | solution.py:593
  8.2 8.0 %collective-permute-start.2 = (bf16[40,1024]{1,0:T(8,128)(2,1)S(1)}, bf16[40,1024]{1,0:T(8,128)(2,1)S(1)}, u32[]{:S(2)}, u32[]{:S(2)}) collective-permute-start(bf16[40,1024]{1,0:T(8,128)(2,1)S(1)} %shard_map.154._.a_ref.refs_0_.refs_14_), channel_id=1, source_target_pairs={{0,4},{1,5},{2,6},{3,7},{4,0},{5,1},{6,2},{7,3},{8,12},{9,13},{10,... | collective-permute-start | bytes 245768 | tf_op jit(solution)/shard_map/ppermute | solution.py:593
  10.8 6.4 %collective-permute-start.1 = (bf16[40,1024]{1,0:T(8,128)(2,1)S(1)}, bf16[40,1024]{1,0:T(8,128)(2,1)S(1)}, u32[]{:S(2)}, u32[]{:S(2)}) collective-permute-start(bf16[40,1024]{1,0:T(8,128)(2,1)S(1)} %shard_map.154._.a_ref.refs_0_.refs_14_), channel_id=1, source_target_pairs={{0,6},{1,7},{2,4},{3,5},{4,2},{5,3},{6,0},{7,1},{8,14},{9,15},{10,... | collective-permute-start | bytes 245768 | tf_op jit(solution)/shard_map/ppermute | solution.py:593
  15.3 7.2 %collective-permute-start.4 = (bf16[80,1024]{1,0:T(8,128)(2,1)S(1)}, bf16[80,1024]{1,0:T(8,128)(2,1)S(1)}, u32[]{:S(2)}, u32[]{:S(2)}) collective-permute-start(bf16[80,1024]{1,0:T(8,128)(2,1)S(1)} %shard_map.158), channel_id=1, source_target_pairs={{0,2},{1,3},{2,0},{3,1},{4,6},{5,7},{6,4},{7,5},{8,10},{9,11},{10,... | collective-permute-start | bytes 491528 | tf_op jit(solution)/shard_map/ppermute | solution.py:593
  17.2 5.2 %collective-permute-start.6 = (bf16[40,1024]{1,0:T(8,128)(2,1)S(1)}, bf16[40,1024]{1,0:T(8,128)(2,1)S(1)}, u32[]{:S(2)}, u32[]{:S(2)}) collective-permute-start(bf16[40,1024]{1,0:T(8,128)(2,1)S(1)} %get-tuple-element.72.refs_5_.refs_19_), channel_id=1, source_target_pairs={{0,1},{1,0},{2,3},{3,2},{4,5},{5,4},{6,7},{7,6},{8,9},{9,8},{10,11... | collective-permute-start | bytes 245768 | tf_op jit(solution)/shard_map/ppermute | solution.py:593
  17.7 4.8 %collective-permute-start.5 = (bf16[40,1024]{1,0:T(8,128)(2,1)S(1)}, bf16[40,1024]{1,0:T(8,128)(2,1)S(1)}, u32[]{:S(2)}, u32[]{:S(2)}) collective-permute-start(bf16[40,1024]{1,0:T(8,128)(2,1)S(1)} %get-tuple-element.64._.refs_3_.refs_17_), channel_id=1, source_target_pairs={{0,1},{1,0},{2,3},{3,2},{4,5},{5,4},{6,7},{7,6},{8,9},{9,8},{10,11... | collective-permute-start | bytes 245768 | tf_op jit(solution)/shard_map/ppermute | solution.py:593
  22.5 1.4 %collective-permute-start.7 = (bf16[64,1024]{1,0:T(8,128)(2,1)S(1)}, bf16[64,1024]{1,0:T(8,128)(2,1)S(1)}, u32[]{:S(2)}, u32[]{:S(2)}) collective-permute-start(bf16[64,1024]{1,0:T(8,128)(2,1)S(1)} %shard_map.159.refs_21_), channel_id=1, source_target_pairs={{0,8},{8,0},{16,24},{24,16},{1,9},{9,1},{17,25},{25,17},{2,10},{10... | collective-permute-start | bytes 393224 | tf_op jit(solution)/shard_map/ppermute | solution.py:593
  31.8 1.4 %collective-permute-start.8 = (bf16[64,1024]{1,0:T(8,128)(2,1)S(1)}, bf16[64,1024]{1,0:T(8,128)(2,1)S(1)}, u32[]{:S(2)}, u32[]{:S(2)}) collective-permute-start(bf16[64,1024]{1,0:T(8,128)(2,1)S(1)} %get-tuple-element.74), channel_id=1, source_target_pairs={{0,8},{8,0},{16,24},{24,16},{1,9},{9,1},{17,25},{25,17},{2,10},{10... | collective-permute-start | bytes 393224 | tf_op jit(solution)/shard_map/ppermute | solution.py:593
  33.3 9.4 %collective-permute-start.9 = (bf16[80,1024]{1,0:T(8,128)(2,1)S(1)}, bf16[80,1024]{1,0:T(8,128)(2,1)S(1)}, u32[]{:S(2)}, u32[]{:S(2)}) collective-permute-start(bf16[80,1024]{1,0:T(8,128)(2,1)S(1)} %get-tuple-element.91), channel_id=1, source_target_pairs={{0,2},{1,3},{2,0},{3,1},{4,6},{5,7},{6,4},{7,5},{8,10},{9,11},{10,... | collective-permute-start | bytes 491528 | tf_op jit(solution)/shard_map/ppermute | solution.py:593
  34.6 5.1 %collective-permute-start.10 = (bf16[40,1024]{1,0:T(8,128)(2,1)S(1)}, bf16[40,1024]{1,0:T(8,128)(2,1)S(1)}, u32[]{:S(2)}, u32[]{:S(2)}) collective-permute-start(bf16[40,1024]{1,0:T(8,128)(2,1)S(1)} %get-tuple-element.93), channel_id=1, source_target_pairs={{0,1},{1,0},{2,3},{3,2},{4,5},{5,4},{6,7},{7,6},{8,9},{9,8},{10,11... | collective-permute-start | bytes 245768 | tf_op jit(solution)/shard_map/ppermute | solution.py:593
  35.7 6.9 %collective-permute-start.12 = (bf16[40,1024]{1,0:T(8,128)(2,1)S(1)}, bf16[40,1024]{1,0:T(8,128)(2,1)S(1)}, u32[]{:S(2)}, u32[]{:S(2)}) collective-permute-start(bf16[40,1024]{1,0:T(8,128)(2,1)S(1)} %get-tuple-element.95), channel_id=1, source_target_pairs={{0,1},{1,0},{2,3},{3,2},{4,5},{5,4},{6,7},{7,6},{8,9},{9,8},{10,11... | collective-permute-start | bytes 245768 | tf_op jit(solution)/shard_map/ppermute | solution.py:593
  39.7 6.7 %collective-permute-start.11 = (bf16[40,1024]{1,0:T(8,128)(2,1)S(1)}, bf16[40,1024]{1,0:T(8,128)(2,1)S(1)}, u32[]{:S(2)}, u32[]{:S(2)}) collective-permute-start(bf16[40,1024]{1,0:T(8,128)(2,1)S(1)} %shard_map.164), channel_id=1, source_target_pairs={{0,6},{1,7},{2,4},{3,5},{4,2},{5,3},{6,0},{7,1},{8,14},{9,15},{10,... | collective-permute-start | bytes 245768 | tf_op jit(solution)/shard_map/ppermute | solution.py:593
  42.6 6.3 %collective-permute-start.13 = (bf16[40,1024]{1,0:T(8,128)(2,1)S(1)}, bf16[40,1024]{1,0:T(8,128)(2,1)S(1)}, u32[]{:S(2)}, u32[]{:S(2)}) collective-permute-start(bf16[40,1024]{1,0:T(8,128)(2,1)S(1)} %shard_map.165), channel_id=1, source_target_pairs={{0,4},{1,5},{2,6},{3,7},{4,0},{5,1},{6,2},{7,3},{8,12},{9,13},{10,... | collective-permute-start | bytes 245768 | tf_op jit(solution)/shard_map/ppermute | solution.py:593
  42.8 6.2 %collective-permute-start.14 = (bf16[40,1024]{1,0:T(8,128)(2,1)S(1)}, bf16[40,1024]{1,0:T(8,128)(2,1)S(1)}, u32[]{:S(2)}, u32[]{:S(2)}) collective-permute-start(bf16[40,1024]{1,0:T(8,128)(2,1)S(1)} %shard_map.166), channel_id=1, source_target_pairs={{0,1},{1,0},{2,3},{3,2},{4,5},{5,4},{6,7},{7,6},{8,9},{9,8},{10,11... | collective-permute-start | bytes 245768 | tf_op jit(solution)/shard_map/ppermute | solution.py:593
  49.0 3.8 %collective-permute-start.15 = (f32[4,1024]{1,0:T(4,128)S(1)}, f32[4,1024]{1,0:T(4,128)S(1)}, u32[]{:S(2)}, u32[]{:S(2)}) collective-permute-start(f32[4,1024]{1,0:T(4,128)S(1)} %get-tuple-element.100), channel_id=1, source_target_pairs={{0,16},{8,24},{16,0},{24,8},{1,17},{9,25},{17,1},{25,9},{2,18},{10... | collective-permute-start | bytes 49160 | tf_op jit(solution)/shard_map/ppermute | solution.py:593

commit v2 on v1

--- a/solution.py
+++ b/solution.py
@@ -108,20 +108,29 @@
 
 def places(slots):
     if slots < 4:
-        return [(s, 0) for s in range(slots)]
-    return [(0, 0), (1, 0), (2, 0), (2, 1)] + [(s - 1, 0) for s in range(4, slots)]
+        return [(s, None) for s in range(slots)]
+    found = [(0, None), (1, None), (2, 0), (2, 1)]
+    for n in range(3, 3 * slots // 4, 3):
+        found += [(n, None), (n + 2, 0), (n + 1, None), (n + 2, 1)]
+    return found
+
+
+def arrays_of(slots):
+    return max(i for i, _ in places(slots)) + 1
 
 
 def terms_kernel(slots, mid_part, where_ref, mid_len_ref, leaf_len_ref, *refs):
     own_parts = refs[:7], refs[7:14]
-    arrays = places(slots)[-1][0] + 1
-    block_refs = [refs[14 + i].at[pl.ds(j * 2 * mid_part, 2 * mid_part)] for i, j in places(slots)]
+    arrays = arrays_of(slots)
+    block_refs = [
+        refs[14 + i].at[pl.ds((j or 0) * 2 * mid_part, 2 * mid_part)] for i, j in places(slots)
+    ]
     root_refs = refs[14 + arrays : 16 + arrays]
     outs = refs[16 + arrays :]
-    keys_ref, ds_ref, dk_ref, dv_ref = outs[:4]
-    dmid_refs = outs[4 : 4 + slots]
-    droot_refs = outs[4 + slots : 6 + slots]
-    s_refs, dp_refs, p_refs = (outs[6 + slots + 2 * i : 8 + slots + 2 * i] for i in range(3))
+    keys_ref, ds_ref, own_p_ref = outs[:3]
+    dmid_refs = outs[3 : 3 + slots]
+    droot_refs = outs[3 + slots : 5 + slots]
+    s_refs, dp_refs, p_refs = (outs[5 + slots + 2 * i : 7 + slots + 2 * i] for i in range(3))
     root_half = root_refs[0].shape[0] // 2
     me = where_ref[0]
     mid_live = mid_len_ref[0]
@@ -198,31 +207,29 @@
             rd = rd * inv
             at = part * sizes[0]
 
-            def finish(to, e, dp, scale):
+            def finish(at, e, dp, scale, p_out, p_at):
                 p = e * scale
-                p_ref[to : to + CHUNK] = p.astype(jnp.bfloat16)
-                ds_ref[self.h, at + to : at + to + CHUNK] = (p * (dp - rd)).astype(jnp.bfloat16)
+                p_out[p_at : p_at + CHUNK] = p.astype(jnp.bfloat16)
+                ds_ref[self.h, at : at + CHUNK] = (p * (dp - rd)).astype(jnp.bfloat16)
 
             for r in starts:
-                finish(r, s_ref[r : r + CHUNK], dp_ref[r : r + CHUNK], inv)
+                finish(at + r, s_ref[r : r + CHUNK], dp_ref[r : r + CHUNK], inv, p_ref, r)
             own = own * inv
             for r in range(0, (part + 1) * half, CHUNK):
-                source = slice(part * half + r, part * half + r + CHUNK)
-                finish(shared + r, self.e_ref[self.i, source], self.own_dp_ref[self.i, source], own)
+                to = part * half + r
+                source = slice(to, to + CHUNK)
+                e, dp = self.e_ref[self.i, source], self.own_dp_ref[self.i, source]
+                finish(at + shared + r, e, dp, own, own_p_ref.at[self.h], to)
 
         def grads(self, part):
-            n = sizes[part]
             at = part * sizes[0]
-            self.dv[part] = dot(p_refs[part][:n], self.gs[part], NN)
-            self.dk[part] = dot(ds_ref[self.h, at : at + n], self.qs[part], NN)
+            self.dv[part] = dot(p_refs[part][...], self.gs[part], NN)
+            self.dk[part] = dot(ds_ref[self.h, at : at + shared], self.qs[part], NN)
 
         def finish(self):
-            m = sizes[0]
-            dk, dv = (jnp.concatenate([x[0] + x[1][:m], x[1][m:]], 0) for x in (self.dk, self.dv))
-            dk = dk * FACTOR
+            dv = self.dv[0] + self.dv[1]
+            dk = (self.dk[0] + self.dk[1]) * FACTOR
             at = self.at
-            dk_ref[:, at] = dk[shared:].astype(jnp.bfloat16)
-            dv_ref[:, at] = dv[shared:].astype(jnp.bfloat16)
             for i, o in enumerate(droot_refs):
                 r = slice(i * root_half, (i + 1) * root_half)
                 o[:, at] = jnp.concatenate([dk[r], dv[r]], 0).astype(jnp.bfloat16)
@@ -249,15 +256,10 @@
         b.finish()
 
 
-def query_grads_kernel(heads_per, first, count, half, carried, _, keys_ref, ds_ref, *refs):
-    dq_hbm, dq_ref, sems, carried_sems = refs[-4 - carried], *refs[-3:]
+def query_grads_kernel(heads_per, first, count, half, _, keys_ref, ds_ref, *refs):
+    dq_hbm, dq_ref, sems = refs[-3:]
     n_all = keys_ref.shape[1]
     span = heads_per * HD
-    moves = [
-        pltpu.make_async_copy(refs[i], refs[i - 3 - carried], carried_sems.at[i]) for i in range(carried)
-    ]
-    for c in moves:
-        c.start()
 
     def copy_out(i):
         at = pl.ds(pl.multiple_of(i * span, span), span)
@@ -278,10 +280,45 @@
                 dq_ref[part * half : (part + 1) * half, at] = dq[g * half : (g + 1) * half]
         copy_out(i).start()
 
-    for c in moves:
-        c.wait()
     for i in range(count):
         copy_out(i).wait()
+
+
+def own_grads_kernel(_, q0_ref, g0_ref, q1_ref, g1_ref, p_ref, ds_ref, dk_hbm, dv_hbm, dk_ref, dv_ref, sems):
+    pairs, leaf_rows, span = q0_ref.shape
+    half = leaf_rows // 2
+    heads_per = span // HD
+    first = ds_ref.shape[1] // 2 - half // 2
+
+    def copies_out(h):
+        at = pl.ds(pl.multiple_of(h * HD, HD), HD)
+        return [
+            pltpu.make_async_copy(x.at[:, at], y.at[:, at], sems.at[h, j])
+            for j, (x, y) in enumerate(((dk_ref, dk_hbm), (dv_ref, dv_hbm)))
+        ]
+
+    @pl.loop(0, pairs)
+    def two_heads(i):
+        for parity, (q_ref, g_ref) in enumerate(((q0_ref, g0_ref), (q1_ref, g1_ref))):
+            h = 2 * i + parity
+            at = pl.ds(pl.multiple_of(h * HD, HD), HD)
+            dk, dv = [], []
+            for part in range(2):
+                n = (part + 1) * half
+                end = first if part == 0 else ds_ref.shape[1]
+                qs = stacked(q_ref.at[i], part, half, heads_per)
+                gs = stacked(g_ref.at[i], part, half, heads_per)
+                dv.append(dot(p_ref[h, part * half : part * half + n], gs, NN))
+                dk.append(dot(ds_ref[h, end - n : end], qs, NN))
+            for x, ref, scale in ((dk, dk_ref, FACTOR), (dv, dv_ref, 1.0)):
+                ref[:half, at] = ((x[0] + x[1][:half]) * scale).astype(jnp.bfloat16)
+                ref[half:, at] = (x[1][half:] * scale).astype(jnp.bfloat16)
+            for c in copies_out(h):
+                c.start()
+
+    for h in range(2 * pairs):
+        for c in copies_out(h):
+            c.wait()
 
 
 def cost(matmuls, key_rows, queries, nbytes):
@@ -333,8 +370,7 @@
     shapes = [
         (heads, key_rows, HD),
         (heads, 2 * key_rows - half, lanes),
-        (leaf_rows, cols),
-        (leaf_rows, cols),
+        (heads, 3 * half, lanes),
     ]
     shapes += [(2 * mid_part, cols)] * slots + [x.shape for x in roots]
     out = pl.pallas_call(
@@ -343,38 +379,53 @@
         out_specs=[VMEM] * len(shapes),
         out_shape=[jax.ShapeDtypeStruct(s, bf) for s in shapes],
         scratch_shapes=[pltpu.VMEM((shared, lanes), f32) for _ in range(4)]
-        + [pltpu.VMEM((key_rows, lanes), bf) for _ in range(2)],
-        compiler_params=pltpu.CompilerParams(vmem_limit_bytes=(14 if shared <= 256 else 40) << 20),
+        + [pltpu.VMEM((shared, lanes), bf) for _ in range(2)],
+        compiler_params=pltpu.CompilerParams(vmem_limit_bytes=(14 if shared <= 256 else 52) << 20),
         cost_estimate=pl.CostEstimate(
             flops=8 * leaf_rows * key_rows * span * heads,
             bytes_accessed=4 * leaf_rows * span * heads,
             transcendentals=leaf_rows * key_rows * heads,
         ),
     )(where, mid_len, leaf_len, *own[0], *own[1], *blocks, *roots)
-    return out[0], out[1], out[2:4], out[4 : 4 + slots], out[4 + slots :]
-
-
-def query_grads(after_this, first, count, so_far, queries, keys, ds, carried=()):
+    return out[0], out[1], out[2], out[3 : 3 + slots], out[3 + slots :]
+
+
+def query_grads(after_this, first, count, so_far, queries, keys, ds):
     rows, cols = queries.shape
     heads = keys.shape[0]
     heads_per = cols // (heads * HD)
-    like = [jax.ShapeDtypeStruct(x.shape, x.dtype) for x in (queries, *carried)]
-    return pl.pallas_call(
-        functools.partial(query_grads_kernel, heads_per, first, count, rows // 2, len(carried)),
-        in_specs=[ANY] + [VMEM] * (2 + len(carried)) + [ANY] * len(so_far),
-        out_specs=[ANY] * len(like),
-        out_shape=like,
-        input_output_aliases={3 + len(carried) + i: i for i in range(len(so_far))},
+    return pl.pallas_call(
+        functools.partial(query_grads_kernel, heads_per, first, count, rows // 2),
+        in_specs=[ANY] + [VMEM] * 2 + [ANY] * len(so_far),
+        out_specs=ANY,
+        out_shape=jax.ShapeDtypeStruct(queries.shape, jnp.bfloat16),
+        input_output_aliases={3 + i: i for i in range(len(so_far))},
         scratch_shapes=[
             pltpu.VMEM((rows, count * heads_per * HD), jnp.bfloat16),
             pltpu.SemaphoreType.DMA((count,)),
-            pltpu.SemaphoreType.DMA((max(len(carried), 1),)),
         ],
         compiler_params=pltpu.CompilerParams(
             vmem_limit_bytes=(10 if keys.shape[1] <= 512 else 32) << 20
         ),
         cost_estimate=cost(1, keys.shape[1] * count // heads, queries, 2 * queries.size),
-    )(after_this, keys, ds, *carried, *so_far)
+    )(after_this, keys, ds, *so_far)
+
+
+def own_grads(after_this, queries, leaf_keys, own, p, ds):
+    heads = p.shape[0]
+    shape = jax.ShapeDtypeStruct(leaf_keys.shape, jnp.bfloat16)
+    return pl.pallas_call(
+        own_grads_kernel,
+        in_specs=[ANY] + [VMEM] * 6,
+        out_specs=[ANY] * 2,
+        out_shape=[shape] * 2,
+        scratch_shapes=[pltpu.VMEM(shape.shape, shape.dtype)] * 2
+        + [pltpu.SemaphoreType.DMA((heads, 2))],
+        compiler_params=pltpu.CompilerParams(
+            vmem_limit_bytes=(10 if ds.shape[1] <= 1024 else 52) << 20
+        ),
+        cost_estimate=cost(2, leaf_keys.shape[0], queries, 2 * queries.size),
+    )(*in_hbm(after_this), *own[0][:2], *own[1][:2], p, ds)
 
 
 def gather_kernel(mk_ref, mv_ref, rk_ref, rv_ref, mid_ref, pair_ref):
@@ -435,14 +486,9 @@
     return both[place * rows : (place + 1) * rows]
 
 
-def two_level(slots):
-    found = places(slots)
-    return [(i, j if slots >= 4 and i == 2 else None) for i, j in found]
-
-
 def collect_kernel(slots, mid_rows, _, *refs):
     out_ref = refs[-1]
-    roots = [root_of(refs[i], mid_rows, j) for i, j in two_level(slots)]
+    roots = [root_of(refs[i], mid_rows, j) for i, j in places(slots)]
     half = roots[0].shape[0] // 2
     out_ref[...] = jnp.concatenate(
         [r[:half] for r in roots] + [r[half:] for r in roots], 0
@@ -459,7 +505,7 @@
     )(first, *blocks)
 
 
-def spread_kernel(slots, mid_rows, a_ref, b_ref, *refs):
+def spread_kernel(slots, mid_rows, _, a_ref, b_ref, *refs):
     mids, outs = refs[:slots], refs[slots:]
     total = a_ref[...].astype(jnp.float32) + b_ref[...].astype(jnp.float32)
     half = total.shape[0] // 2
@@ -469,7 +515,7 @@
         for s in range(slots)
     ]
     held = {}
-    for s, (i, j) in enumerate(two_level(slots)):
+    for s, (i, j) in enumerate(places(slots)):
         at = mid_rows * (j or 0)
         outs[i][at : at + mid_rows] = mids[s][...]
         held.setdefault(i, []).append(roots[s])
@@ -477,60 +523,52 @@
         outs[i][len(x) * mid_rows :] = jnp.concatenate(x, 0).astype(jnp.bfloat16)
 
 
-def spread(a, b, mids):
+def spread(first, a, b, mids):
     slots = len(mids)
     mid_rows, cols = mids[0].shape
     rows = mid_rows + a.shape[0] // slots
-    arrays = places(slots)[-1][0] + 1
-    shapes = [(2 * rows if slots >= 4 and i == 2 else rows, cols) for i in range(arrays)]
+    arrays = arrays_of(slots)
+    paired = {i for i, j in places(slots) if j is not None}
+    shapes = [(2 * rows if i in paired else rows, cols) for i in range(arrays)]
     return pl.pallas_call(
         functools.partial(spread_kernel, slots, mid_rows),
+        in_specs=[ANY] + [VMEM] * (2 + slots),
         out_shape=[jax.ShapeDtypeStruct(x, jnp.bfloat16) for x in shapes],
         compiler_params=pltpu.CompilerParams(vmem_limit_bytes=8 << 20),
-    )(a, b, *mids)
-
-
-def near_sum_kernel(mid_rows, a_ref, pair_ref, out_ref):
+    )(*in_hbm(first), a, b, *mids)
+
+
+def near_sum_kernel(mid_rows, _, a_ref, pair_ref, out_ref):
     pair = pair_ref[mid_rows : 2 * mid_rows].astype(jnp.float32)
     out_ref[:mid_rows] = (a_ref[:mid_rows].astype(jnp.float32) + pair).astype(jnp.bfloat16)
     root = root_of(a_ref, mid_rows, None) + root_of(pair_ref, mid_rows, 1)
     out_ref[mid_rows:] = root.astype(jnp.bfloat16)
 
 
-def near_sum(a, pair, mid_rows):
+def near_sum(first, a, pair, mid_rows):
     return pl.pallas_call(
         functools.partial(near_sum_kernel, mid_rows),
-        out_shape=jax.ShapeDtypeStruct(a.shape, a.dtype),
-        compiler_params=pltpu.CompilerParams(vmem_limit_bytes=4 << 20),
-    )(a, pair)
-
-
-def far_sum_kernel(_, a_ref, b_ref, out_ref):
-    out_ref[...] = (a_ref[...].astype(jnp.float32) + b_ref[...].astype(jnp.float32)).astype(jnp.bfloat16)
-
-
-def far_sum(first, a, b):
-    return pl.pallas_call(
-        far_sum_kernel,
         in_specs=[ANY] + [VMEM] * 2,
         out_shape=jax.ShapeDtypeStruct(a.shape, a.dtype),
         compiler_params=pltpu.CompilerParams(vmem_limit_bytes=4 << 20),
-    )(first, a, b)
-
-
-def after_kernel(*refs):
-    pass
-
-
-def after(first, arrays):
-    return pl.pallas_call(
-        after_kernel,
-        in_specs=[VMEM] + [ANY] * len(arrays),
-        out_specs=[ANY] * len(arrays),
-        out_shape=[jax.ShapeDtypeStruct(x.shape, x.dtype) for x in arrays],
-        input_output_aliases={1 + i: i for i in range(len(arrays))},
-        compiler_params=pltpu.CompilerParams(vmem_limit_bytes=4 << 20),
-    )(first, *arrays)
+    )(first, a, pair)
+
+
+def far_sums_kernel(mid_rows, _, a_ref, b_ref, pair_ref, *outs):
+    for j, (x, o) in enumerate(zip((a_ref, b_ref), outs)):
+        mid = pair_ref[j * mid_rows : (j + 1) * mid_rows].astype(jnp.float32)
+        o[:mid_rows] = (x[:mid_rows].astype(jnp.float32) + mid).astype(jnp.bfloat16)
+        root = root_of(x, mid_rows, None) + root_of(pair_ref, mid_rows, j)
+        o[mid_rows:] = root.astype(jnp.bfloat16)
+
+
+def far_sums(first, a, b, pair, mid_rows):
+    return pl.pallas_call(
+        functools.partial(far_sums_kernel, mid_rows),
+        in_specs=[ANY] + [VMEM] * 3,
+        out_shape=[jax.ShapeDtypeStruct(x.shape, x.dtype) for x in (a, b)],
+        compiler_params=pltpu.CompilerParams(vmem_limit_bytes=8 << 20),
+    )(*in_hbm(first), a, b, pair)
 
 
 def mid_sums_kernel(mid_part, *refs):
@@ -619,38 +657,48 @@
     def leaf_swap(x, s):
         return swap(x, "leaf", leaves, s)
 
-    far = list(reversed(range(4, leaves, 2)))
-    far_blocks = [leaf_swap(block, s) for s in far]
+    far = [s for f in range(4, leaves, 4) for s in (f + 2, f)]
+    far_blocks = {s: leaf_swap(block, s) for s in far}
     beside = leaf_swap(block, 1)
     operands = (queries, out_grad, leaf_keys, leaf_values)
     own = [own_part(0, block, *operands)]
     token = own[0][-1]
-    near = leaf_swap(join(token, block, beside, mid_rows), 2)
-    far_blocks = after(token, far_blocks)
-    own.append(own_part(1, far_blocks[-1] if far else token, *operands))
-    blocks = [block, beside, near]
-    for x in reversed(far_blocks):
-        blocks += [x, leaf_swap(x, 1)]
+    blocks = [block, beside]
+    if leaves >= 4:
+        blocks.append(leaf_swap(join(token, block, beside, mid_rows), 2))
+    for f in range(4, leaves, 4):
+        x, y = far_blocks[f], far_blocks[f + 2]
+        both = join(token, x, y, mid_rows)
+        token = both
+        blocks += [x, y, leaf_swap(both, 1)]
+    own.append(own_part(1, token, *operands))
     root = collect(own[1][-1], blocks, leaves, mid_rows)
     roots = [root, swap(root, "mid", mids, 1)]
-    keys, ds, leaf_grads, mid_terms, root_terms = terms_part(
+    keys, ds, own_p, mid_terms, root_terms = terms_part(
         where, mid_len, leaf_len, leaves, own, blocks, roots, mid_part
     )
 
-    terms = spread(root_terms[0], swap(root_terms[1], "mid", mids, 1), mid_terms)
-    through = [leaf_swap(terms[s], 1) for s in far]
-    near = leaf_swap(terms[2], 2)
     heads = leaf_keys.shape[1] // HD
-    early = heads // 2
-    query_grad, *leaf_grads = query_grads(terms[0], 0, early, (), queries, keys, ds, leaf_grads)
-    leaf_key_grad, leaf_value_grad = leaf_grads
-    token = in_hbm(leaf_value_grad)[0]
-    arrived = [terms[0], near]
-    for s, x in zip(far, through):
-        arrived.append(leaf_swap(far_sum(token, terms[s - 1], x), s))
-    arrived.append(leaf_swap(near_sum(terms[1], near, mid_rows), 1))
-    (query_grad,) = query_grads(terms[0], early, heads - early, (query_grad,), queries, keys, ds)
-    pieces = root_sums(query_grad, arrived, mid_rows, root_own, mids // 2)
+    cuts = [0, heads // 4, heads]
+
+    def query_part(first, i, so_far):
+        return query_grads(first, cuts[i], cuts[i + 1] - cuts[i], so_far, queries, keys, ds)
+
+    query_grad = query_part(where, 0, ())
+    terms = spread(query_grad, root_terms[0], swap(root_terms[1], "mid", mids, 1), mid_terms)
+    through = {f: leaf_swap(terms[3 * f // 4 + 2], 1) for f in range(4, leaves, 4)}
+    query_grad = query_part(terms[0], 1, (query_grad,))
+    near = leaf_swap(terms[2], 2) if leaves >= 4 else None
+    arrived = [terms[0]] if near is None else [terms[0], near]
+    last = terms[0]
+    for f, x in through.items():
+        n = 3 * f // 4
+        a, last = far_sums(query_grad, terms[n], terms[n + 1], x, mid_rows)
+        arrived += [leaf_swap(last, f + 2), leaf_swap(a, f)]
+    beside = terms[1] if near is None else near_sum(last, terms[1], near, mid_rows)
+    arrived.append(leaf_swap(beside, 1))
+    leaf_key_grad, leaf_value_grad = own_grads(query_grad, queries, leaf_keys, own, own_p, ds)
+    pieces = root_sums(leaf_value_grad, arrived, mid_rows, root_own, mids // 2)
     mid_key_grad, mid_value_grad = mid_sums(arrived, mid_part)
     pieces = [pieces[0]] + [swap(x, "mid", mids, t) for t, x in zip(same_core, pieces[1:])]
     root_key_grad, root_value_grad = add_roots(pieces)

time: 53.7 us -> 53.9 us (level)
  starting transfers between devices: 20.7 us -> 15.4 us
  waiting for transfers between devices: 9.42 us -> 13 us
  Pallas kernels: 21.3 us -> 23.2 us
    ppermute x16 -> x14, starting transfers between devices: 20.7 us -> 15.4 us  [swap(): return lax.ppermute(x, axis, [(i, i ^ offset) for i in range(size)])]
    ppermute x16 -> x14, waiting for transfers between devices: 9.42 us -> 13 us  [swap(): return lax.ppermute(x, axis, [(i, i ^ offset) for i in range(size)])]
    pallas_call x5 -> x4, Pallas kernels: 0.15 us -> 3.17 us  [the longest x1 3.02 us: own_grads(): pl.pallas_call(own_grads_kernel, in_specs=[ANY] + [VMEM] * 6, out_specs=[...]
    pallas_call x1, Pallas kernels: 7.87 us -> 6.81 us  [terms_part(): pl.pallas_call(functools.partial(terms_kernel, slots, mid_part), in_specs...]
  transfers between devices with their start and end apart: 16 -> 14, of which waited for: 9 -> 8; matrix products, arithmetic and copies ran while one was open for 0% -> 0% of each run, Pallas kernels for 22% -> 28%
where the time goes in v2:
time: 53.9 us; the launch traced here: 53.7 us
  Pallas kernels  23.2 us (43%)
  starting transfers between devices  15.4 us (29%)
  waiting for transfers between devices  13 us (24%)
  between operations  2.06 us (4%)
    ppermute x14, starting transfers between devices, swap(): return lax.ppermute(x, axis, [(i, i ^ offset) for i in range(size)])  15.4 us
    ppermute x14, waiting for transfers between devices, swap(): return lax.ppermute(x, axis, [(i, i ^ offset) for i in range(size)])  13 us
    pallas_call x1, Pallas kernels, terms_part(): pl.pallas_call(functools.partial(terms_kernel, slots, mid_part), in_specs...  6.81 us
    pallas_call x2, Pallas kernels, own_part(): pl.pallas_call(functools.partial(own_kernel, parity), in_specs=[ANY] * 5,...  6.27 us
    pallas_call x2, Pallas kernels, query_grads(): pl.pallas_call(functools.partial(query_grads_kernel, heads_per, first, co...  4.8 us
    pallas_call x1, Pallas kernels, own_grads(): pl.pallas_call(own_grads_kernel, in_specs=[ANY] + [VMEM] * 6, out_specs=[...  3.02 us
  transfers between devices with their start and end apart: 14, of which 8 were waited for; matrix products, arithmetic and copies ran while one was open for 0% of the time, Pallas kernels for 28%

profile of v2, /device:TPU:0, one launch (start us, length us, event | category | flops | bytes accessed | tf_op | source)
XLA Modules:
  0.0 53.7 jit_solution(14251397584246637598)
XLA Ops:
  0.6 0.8 %shard_map.153 = (bf16[32,1024]{1,0:T(8,128)(2,1)S(1)}, bf16[4,1024]{1,0:T(4,128)(2,1)S(1)}) custom-call(bf16[16,1024]{1,0:T(8,128)(2,1)} %mk_ref.1, bf16[16,1024]{1,0:T(8,128)(2,1)} %mv_ref.1, bf16[2,1024]{1,0:T(2,128)(2,1)} %rk_ref.1, bf16[2,1024]{1,0:T(2,128)(2,1)} %rv_ref.1), custom_call_target="tpu_custom_call" | custom-call | tf_op jit(solution)/shard_map/pallas_call | solution.py:437
  1.4 3.0 %collective-permute-start = (bf16[4,1024]{1,0:T(4,128)(2,1)S(1)}, bf16[4,1024]{1,0:T(4,128)(2,1)S(1)}, u32[]{:S(2)}, u32[]{:S(2)}) collective-permute-start(bf16[4,1024]{1,0:T(4,128)(2,1)S(1)} %get-tuple-element.53.refs_0_), channel_id=1, source_target_pairs={{0,16},{8,24},{16,0},{24,8},{1,17},{9,25},{17,1},{25,9},{2,18},{10... | collective-permute-start | bytes 24584 | tf_op jit(solution)/shard_map/ppermute | solution.py:631
  5.8 0.3 collective-permute-done.refs_1_
  6.1 2.1 %collective-permute-start.3 = (bf16[40,1024]{1,0:T(8,128)(2,1)S(1)}, bf16[40,1024]{1,0:T(8,128)(2,1)S(1)}, u32[]{:S(2)}, u32[]{:S(2)}) collective-permute-start(bf16[40,1024]{1,0:T(8,128)(2,1)S(1)} %shard_map.154._.a_ref.refs_0_.refs_14_), channel_id=1, source_target_pairs={{0,1},{1,0},{2,3},{3,2},{4,5},{5,4},{6,7},{7,6},{8,9},{9,8},{10,11... | collective-permute-start | bytes 245768 | tf_op jit(solution)/shard_map/ppermute | solution.py:631
  8.2 3.6 %collective-permute-start.2 = (bf16[40,1024]{1,0:T(8,128)(2,1)S(1)}, bf16[40,1024]{1,0:T(8,128)(2,1)S(1)}, u32[]{:S(2)}, u32[]{:S(2)}) collective-permute-start(bf16[40,1024]{1,0:T(8,128)(2,1)S(1)} %shard_map.154._.a_ref.refs_0_.refs_14_), channel_id=1, source_target_pairs={{0,6},{1,7},{2,4},{3,5},{4,2},{5,3},{6,0},{7,1},{8,14},{9,15},{10,... | collective-permute-start | bytes 245768 | tf_op jit(solution)/shard_map/ppermute | solution.py:631
  11.8 0.0 collective-permute-start.1
  11.8 3.1 %shard_map.155 = (bf16[4,256,512]{2,1,0:T(8,128)(2,1)S(1)}, bf16[4,256,512]{2,1,0:T(8,128)(2,1)S(1)}, bf16[4,256,128]{2,1,0:T(8,128)(2,1)S(1)}, bf16[4,256,128]{...) custom-call(bf16[40,1024]{1,0:T(8,128)(2,1)S(1)} %shard_map.154._.a_ref.r, ...), custom_call_target="tpu_custom_call" | custom-call | flops 536870912 | bytes 2097152 | tf_op jit(solution)/shard_map/pallas_call | solution.py:350
  14.9 0.0 collective-permute-done.3.b_ref.refs_1_.refs_15_
  14.9 0.9 %collective-permute-start.4 = (bf16[80,1024]{1,0:T(8,128)(2,1)S(1)}, bf16[80,1024]{1,0:T(8,128)(2,1)S(1)}, u32[]{:S(2)}, u32[]{:S(2)}) collective-permute-start(bf16[80,1024]{1,0:T(8,128)(2,1)S(1)} %shard_map.158), channel_id=1, source_target_pairs={{0,2},{1,3},{2,0},{3,1},{4,6},{5,7},{6,4},{7,5},{8,10},{9,11},{10,... | collective-permute-start | bytes 491528 | tf_op jit(solution)/shard_map/ppermute | solution.py:631
  15.8 2.0 %collective-permute-done.1.a_ref.refs_3_.refs_17_ = bf16[40,1024]{1,0:T(8,128)(2,1)S(1)} collective-permute-done((bf16[40,1024]{1,0:T(8,128)(2,1)S(1)}, bf16[40,1024]{1,0:T(8,128)(2,1)S(1)}, u32[]{:S(2)}, u32[]{:S(2)}) %collective-permute-start.1) | collective-permute-done | bytes 81952 | tf_op jit(solution)/shard_map/ppermute | solution.py:631
  17.8 0.6 %collective-permute-start.5 = (bf16[80,1024]{1,0:T(8,128)(2,1)S(1)}, bf16[80,1024]{1,0:T(8,128)(2,1)S(1)}, u32[]{:S(2)}, u32[]{:S(2)}) collective-permute-start(bf16[80,1024]{1,0:T(8,128)(2,1)S(1)} %shard_map.156._), channel_id=1, source_target_pairs={{0,1},{1,0},{2,3},{3,2},{4,5},{5,4},{6,7},{7,6},{8,9},{9,8},{10,11... | collective-permute-start | bytes 491528 | tf_op jit(solution)/shard_map/ppermute | solution.py:631
  18.4 3.2 %shard_map.157 = (bf16[4,256,512]{2,1,0:T(8,128)(2,1)S(1)}, bf16[4,256,512]{2,1,0:T(8,128)(2,1)S(1)}, bf16[4,256,128]{2,1,0:T(8,128)(2,1)S(1)}, bf16[4,256,128]{...) custom-call(bf16[80,1024]{1,0:T(8,128)(2,1)S(1)} %shard_map.156._, ...), custom_call_target="tpu_custom_call" | custom-call | flops 536870912 | bytes 2097152 | tf_op jit(solution)/shard_map/pallas_call | solution.py:350
  21.6 0.0 collective-permute-done.4.refs_2_.refs_16_
  21.6 1.6 %collective-permute-done.5.refs_5_.refs_19_ = bf16[80,1024]{1,0:T(8,128)(2,1)S(1)} collective-permute-done((bf16[80,1024]{1,0:T(8,128)(2,1)S(1)}, bf16[80,1024]{1,0:T(8,128)(2,1)S(1)}, u32[]{:S(2)}, u32[]{:S(2)}) %collective-permute-start.5) | collective-permute-done | bytes 163872 | tf_op jit(solution)/shard_map/ppermute | solution.py:631
  23.3 0.1 collective-permute-start.6
  23.4 1.3 %collective-permute-done.6.refs_21_ = bf16[64,1024]{1,0:T(8,128)(2,1)S(1)} collective-permute-done((bf16[64,1024]{1,0:T(8,128)(2,1)S(1)}, bf16[64,1024]{1,0:T(8,128)(2,1)S(1)}, u32[]{:S(2)}, u32[]{:S(2)}) %collective-permute-start.6) | collective-permute-done | bytes 131104 | tf_op jit(solution)/shard_map/ppermute | solution.py:631
  24.7 6.8 %shard_map.160 = (bf16[8,448,128]{2,1,0:T(8,128)(2,1)S(1)}, bf16[8,768,512]{2,1,0:T(8,128)(2,1)S(1)}, bf16[8,384,512]{2,1,0:T(8,128)(2,1)S(1)}, bf16[32,1024]{1,...) custom-call(s32[1]{0:T(128)} %bitcast.where_ref._, ...), custom_call_target="tpu_custom_call" | custom-call | flops 3758096384 | bytes 4194304 | tf_op jit(solution)/shard_map/pallas_call | solution.py:376
  31.5 0.2 collective-permute-start.7
  31.7 1.6 %shard_map.161._.refs_0_ = bf16[256,4096]{1,0:T(8,128)(2,1)} custom-call(s32[1]{0:T(128)} %bitcast.where_ref._, bf16[8,448,128]{2,1,0:T(8,128)(2,1)S(1)} %get-tuple-element.68.keys_ref, bf16[8,768,512]{2,1,0:T(8,128)(2,1)S(1)} %get-tuple-element.69.ds_ref), custom_call_target="tpu_custom_call" | custom-call | flops 234881024 | bytes 2097152 | tf_op jit(solution)/shard_map/pallas_call | solution.py:397
  33.3 0.1 shard_map.162
  33.4 0.6 %collective-permute-start.9 = (bf16[80,1024]{1,0:T(8,128)(2,1)S(1)}, bf16[80,1024]{1,0:T(8,128)(2,1)S(1)}, u32[]{:S(2)}, u32[]{:S(2)}) collective-permute-start(bf16[80,1024]{1,0:T(8,128)(2,1)S(1)} %get-tuple-element.87), channel_id=1, source_target_pairs={{0,1},{1,0},{2,3},{3,2},{4,5},{5,4},{6,7},{7,6},{8,9},{9,8},{10,11... | collective-permute-start | bytes 491528 | tf_op jit(solution)/shard_map/ppermute | solution.py:631
  34.0 3.3 %shard_map.163._ = bf16[256,4096]{1,0:T(8,128)(2,1)} custom-call(bf16[40,1024]{1,0:T(8,128)(2,1)S(1)} %get-tuple-element.80._.refs_0_, bf16[8,448,128]{2,1,0:T(8,128)(2,1)S(1)} %get-tuple-element.68.keys_ref, bf16[8,768,512]{2,1,0:T(8,128)(2,1)S(1)} %get-tuple-element.69.ds_ref, bf16[256,4096]{1,0:T(8,128)(2,1)} %shard_map.161._.refs_0_), custom_call_target="tpu_custom_call", output_to_operand_aliasing={{}: (3, {})} | custom-call | flops 704643072 | bytes 2097152 | tf_op jit(solution)/shard_map/pallas_call | solution.py:397
  37.2 2.7 %collective-permute-done.9.pair_ref = bf16[80,1024]{1,0:T(8,128)(2,1)S(1)} collective-permute-done((bf16[80,1024]{1,0:T(8,128)(2,1)S(1)}, bf16[80,1024]{1,0:T(8,128)(2,1)S(1)}, u32[]{:S(2)}, u32[]{:S(2)}) %collective-permute-start.9) | collective-permute-done | bytes 163872 | tf_op jit(solution)/shard_map/ppermute | solution.py:631
  40.0 2.2 %collective-permute-start.10 = (bf16[40,1024]{1,0:T(8,128)(2,1)S(1)}, bf16[40,1024]{1,0:T(8,128)(2,1)S(1)}, u32[]{:S(2)}, u32[]{:S(2)}) collective-permute-start(bf16[40,1024]{1,0:T(8,128)(2,1)S(1)} %get-tuple-element.88._), channel_id=1, source_target_pairs={{0,6},{1,7},{2,4},{3,5},{4,2},{5,3},{6,0},{7,1},{8,14},{9,15},{10,... | collective-permute-start | bytes 245768 | tf_op jit(solution)/shard_map/ppermute | solution.py:631
  42.2 0.6 %collective-permute-start.12 = (bf16[40,1024]{1,0:T(8,128)(2,1)S(1)}, bf16[40,1024]{1,0:T(8,128)(2,1)S(1)}, u32[]{:S(2)}, u32[]{:S(2)}) collective-permute-start(bf16[40,1024]{1,0:T(8,128)(2,1)S(1)} %shard_map.166), channel_id=1, source_target_pairs={{0,1},{1,0},{2,3},{3,2},{4,5},{5,4},{6,7},{7,6},{8,9},{9,8},{10,11... | collective-permute-start | bytes 245768 | tf_op jit(solution)/shard_map/ppermute | solution.py:631
  42.8 3.0 %shard_map.164 = (bf16[256,1024]{1,0:T(8,128)(2,1)}, bf16[256,1024]{1,0:T(8,128)(2,1)}) custom-call(bf16[256,4096]{1,0:T(8,128)(2,1)} %shard_map.163._, bf16[4,256,512]{2,1,0:T(8,128)(2,1)S(1)} %get-tuple-element.54.refs_0_.q0_ref, bf16[4,256,512]{2,1,0:T(8,128)(2,1)S(1)} %get-tuple-element.55.refs_1_.g0_ref, ...), custom_call_target="tpu_custom_call" | custom-call | flops 1073741824 | bytes 2097152 | tf_op jit(solution)/shard_map/pallas_call | solution.py:417
  45.9 0.9 %collective-permute-done.12.refs_4_ = bf16[40,1024]{1,0:T(8,128)(2,1)S(1)} collective-permute-done((bf16[40,1024]{1,0:T(8,128)(2,1)S(1)}, bf16[40,1024]{1,0:T(8,128)(2,1)S(1)}, u32[]{:S(2)}, u32[]{:S(2)}) %collective-permute-start.12) | collective-permute-done | bytes 81952 | tf_op jit(solution)/shard_map/ppermute | solution.py:631
  46.7 2.5 %collective-permute-done.11.refs_3_ = bf16[40,1024]{1,0:T(8,128)(2,1)S(1)} collective-permute-done((bf16[40,1024]{1,0:T(8,128)(2,1)S(1)}, bf16[40,1024]{1,0:T(8,128)(2,1)S(1)}, u32[]{:S(2)}, u32[]{:S(2)}) %collective-permute-start.11) | collective-permute-done | bytes 81952 | tf_op jit(solution)/shard_map/ppermute | solution.py:631
  49.3 1.5 %collective-permute-start.13 = (f32[4,1024]{1,0:T(4,128)S(1)}, f32[4,1024]{1,0:T(4,128)S(1)}, u32[]{:S(2)}, u32[]{:S(2)}) collective-permute-start(f32[4,1024]{1,0:T(4,128)S(1)} %get-tuple-element.94), channel_id=1, source_target_pairs={{0,16},{8,24},{16,0},{24,8},{1,17},{9,25},{17,1},{25,9},{2,18},{10... | collective-permute-start | bytes 49160 | tf_op jit(solution)/shard_map/ppermute | solution.py:631
  50.8 0.7 %shard_map.167 = (f32[16,1024]{1,0:T(8,128)}, f32[16,1024]{1,0:T(8,128)}) custom-call(bf16[40,1024]{1,0:T(8,128)(2,1)S(1)} %get-tuple-element.80._.refs_0_, bf16[80,1024]{1,0:T(8,128)(2,1)S(1)} %collective-permute-done.8.pair_ref.refs_1_, bf16[40,1024]{1,0:T(8,128)(2,1)S(1)} %collective-permute-done.10.refs_2_, ...), custom_call_target="tpu_custom_call" | custom-call | tf_op jit(solution)/shard_map/pallas_call | solution.py:584
  51.5 1.6 %collective-permute-done.13.refs_1_ = f32[4,1024]{1,0:T(4,128)S(1)} collective-permute-done((f32[4,1024]{1,0:T(4,128)S(1)}, f32[4,1024]{1,0:T(4,128)S(1)}, u32[]{:S(2)}, u32[]{:S(2)}) %collective-permute-start.13) | collective-permute-done | bytes 16416 | tf_op jit(solution)/shard_map/ppermute | solution.py:631
  53.1 0.6 %shard_map.169 = (f32[2,1024]{1,0:T(2,128)}, f32[2,1024]{1,0:T(2,128)}) custom-call(f32[4,1024]{1,0:T(4,128)S(1)} %get-tuple-element.93.refs_0_, f32[4,1024]{1,0:T(4,128)S(1)} %collective-permute-done.13.refs_1_), custom_call_target="tpu_custom_call" | custom-call | tf_op jit(solution)/shard_map/pallas_call | solution.py:623
  (13 shorter events, 0.2 us)
Async XLA Ops:
  1.4 4.7 %collective-permute-start = (bf16[4,1024]{1,0:T(4,128)(2,1)S(1)}, bf16[4,1024]{1,0:T(4,128)(2,1)S(1)}, u32[]{:S(2)}, u32[]{:S(2)}) collective-permute-start(bf16[4,1024]{1,0:T(4,128)(2,1)S(1)} %get-tuple-element.53.refs_0_), channel_id=1, source_target_pairs={{0,16},{8,24},{16,0},{24,8},{1,17},{9,25},{17,1},{25,9},{2,18},{10... | collective-permute-start | bytes 24584 | tf_op jit(solution)/shard_map/ppermute | solution.py:631
  6.1 8.8 %collective-permute-start.3 = (bf16[40,1024]{1,0:T(8,128)(2,1)S(1)}, bf16[40,1024]{1,0:T(8,128)(2,1)S(1)}, u32[]{:S(2)}, u32[]{:S(2)}) collective-permute-start(bf16[40,1024]{1,0:T(8,128)(2,1)S(1)} %shard_map.154._.a_ref.refs_0_.refs_14_), channel_id=1, source_target_pairs={{0,1},{1,0},{2,3},{3,2},{4,5},{5,4},{6,7},{7,6},{8,9},{9,8},{10,11... | collective-permute-start | bytes 245768 | tf_op jit(solution)/shard_map/ppermute | solution.py:631
  8.2 7.6 %collective-permute-start.2 = (bf16[40,1024]{1,0:T(8,128)(2,1)S(1)}, bf16[40,1024]{1,0:T(8,128)(2,1)S(1)}, u32[]{:S(2)}, u32[]{:S(2)}) collective-permute-start(bf16[40,1024]{1,0:T(8,128)(2,1)S(1)} %shard_map.154._.a_ref.refs_0_.refs_14_), channel_id=1, source_target_pairs={{0,6},{1,7},{2,4},{3,5},{4,2},{5,3},{6,0},{7,1},{8,14},{9,15},{10,... | collective-permute-start | bytes 245768 | tf_op jit(solution)/shard_map/ppermute | solution.py:631
  11.8 6.0 %collective-permute-start.1 = (bf16[40,1024]{1,0:T(8,128)(2,1)S(1)}, bf16[40,1024]{1,0:T(8,128)(2,1)S(1)}, u32[]{:S(2)}, u32[]{:S(2)}) collective-permute-start(bf16[40,1024]{1,0:T(8,128)(2,1)S(1)} %shard_map.154._.a_ref.refs_0_.refs_14_), channel_id=1, source_target_pairs={{0,4},{1,5},{2,6},{3,7},{4,0},{5,1},{6,2},{7,3},{8,12},{9,13},{10,... | collective-permute-start | bytes 245768 | tf_op jit(solution)/shard_map/ppermute | solution.py:631
  14.9 6.7 %collective-permute-start.4 = (bf16[80,1024]{1,0:T(8,128)(2,1)S(1)}, bf16[80,1024]{1,0:T(8,128)(2,1)S(1)}, u32[]{:S(2)}, u32[]{:S(2)}) collective-permute-start(bf16[80,1024]{1,0:T(8,128)(2,1)S(1)} %shard_map.158), channel_id=1, source_target_pairs={{0,2},{1,3},{2,0},{3,1},{4,6},{5,7},{6,4},{7,5},{8,10},{9,11},{10,... | collective-permute-start | bytes 491528 | tf_op jit(solution)/shard_map/ppermute | solution.py:631
  17.8 5.4 %collective-permute-start.5 = (bf16[80,1024]{1,0:T(8,128)(2,1)S(1)}, bf16[80,1024]{1,0:T(8,128)(2,1)S(1)}, u32[]{:S(2)}, u32[]{:S(2)}) collective-permute-start(bf16[80,1024]{1,0:T(8,128)(2,1)S(1)} %shard_map.156._), channel_id=1, source_target_pairs={{0,1},{1,0},{2,3},{3,2},{4,5},{5,4},{6,7},{7,6},{8,9},{9,8},{10,11... | collective-permute-start | bytes 491528 | tf_op jit(solution)/shard_map/ppermute | solution.py:631
  23.3 1.4 %collective-permute-start.6 = (bf16[64,1024]{1,0:T(8,128)(2,1)S(1)}, bf16[64,1024]{1,0:T(8,128)(2,1)S(1)}, u32[]{:S(2)}, u32[]{:S(2)}) collective-permute-start(bf16[64,1024]{1,0:T(8,128)(2,1)S(1)} %shard_map.159.refs_20_), channel_id=1, source_target_pairs={{0,8},{8,0},{16,24},{24,16},{1,9},{9,1},{17,25},{25,17},{2,10},{10... | collective-permute-start | bytes 393224 | tf_op jit(solution)/shard_map/ppermute | solution.py:631
  31.5 1.8 %collective-permute-start.7 = (bf16[64,1024]{1,0:T(8,128)(2,1)S(1)}, bf16[64,1024]{1,0:T(8,128)(2,1)S(1)}, u32[]{:S(2)}, u32[]{:S(2)}) collective-permute-start(bf16[64,1024]{1,0:T(8,128)(2,1)S(1)} %get-tuple-element.71), channel_id=1, source_target_pairs={{0,8},{8,0},{16,24},{24,16},{1,9},{9,1},{17,25},{25,17},{2,10},{10... | collective-permute-start | bytes 393224 | tf_op jit(solution)/shard_map/ppermute | solution.py:631
  33.4 6.5 %collective-permute-start.9 = (bf16[80,1024]{1,0:T(8,128)(2,1)S(1)}, bf16[80,1024]{1,0:T(8,128)(2,1)S(1)}, u32[]{:S(2)}, u32[]{:S(2)}) collective-permute-start(bf16[80,1024]{1,0:T(8,128)(2,1)S(1)} %get-tuple-element.87), channel_id=1, source_target_pairs={{0,1},{1,0},{2,3},{3,2},{4,5},{5,4},{6,7},{7,6},{8,9},{9,8},{10,11... | collective-permute-start | bytes 491528 | tf_op jit(solution)/shard_map/ppermute | solution.py:631
  34.0 8.2 %collective-permute-start.8 = (bf16[80,1024]{1,0:T(8,128)(2,1)S(1)}, bf16[80,1024]{1,0:T(8,128)(2,1)S(1)}, u32[]{:S(2)}, u32[]{:S(2)}) collective-permute-start(bf16[80,1024]{1,0:T(8,128)(2,1)S(1)} %get-tuple-element.84), channel_id=1, source_target_pairs={{0,2},{1,3},{2,0},{3,1},{4,6},{5,7},{6,4},{7,5},{8,10},{9,11},{10,... | collective-permute-start | bytes 491528 | tf_op jit(solution)/shard_map/ppermute | solution.py:631
  40.0 9.3 %collective-permute-start.10 = (bf16[40,1024]{1,0:T(8,128)(2,1)S(1)}, bf16[40,1024]{1,0:T(8,128)(2,1)S(1)}, u32[]{:S(2)}, u32[]{:S(2)}) collective-permute-start(bf16[40,1024]{1,0:T(8,128)(2,1)S(1)} %get-tuple-element.88._), channel_id=1, source_target_pairs={{0,6},{1,7},{2,4},{3,5},{4,2},{5,3},{6,0},{7,1},{8,14},{9,15},{10,... | collective-permute-start | bytes 245768 | tf_op jit(solution)/shard_map/ppermute | solution.py:631
  42.2 4.5 %collective-permute-start.12 = (bf16[40,1024]{1,0:T(8,128)(2,1)S(1)}, bf16[40,1024]{1,0:T(8,128)(2,1)S(1)}, u32[]{:S(2)}, u32[]{:S(2)}) collective-permute-start(bf16[40,1024]{1,0:T(8,128)(2,1)S(1)} %shard_map.166), channel_id=1, source_target_pairs={{0,1},{1,0},{2,3},{3,2},{4,5},{5,4},{6,7},{7,6},{8,9},{9,8},{10,11... | collective-permute-start | bytes 245768 | tf_op jit(solution)/shard_map/ppermute | solution.py:631
  42.8 6.4 %collective-permute-start.11 = (bf16[40,1024]{1,0:T(8,128)(2,1)S(1)}, bf16[40,1024]{1,0:T(8,128)(2,1)S(1)}, u32[]{:S(2)}, u32[]{:S(2)}) collective-permute-start(bf16[40,1024]{1,0:T(8,128)(2,1)S(1)} %get-tuple-element.89), channel_id=1, source_target_pairs={{0,4},{1,5},{2,6},{3,7},{4,0},{5,1},{6,2},{7,3},{8,12},{9,13},{10,... | collective-permute-start | bytes 245768 | tf_op jit(solution)/shard_map/ppermute | solution.py:631
  49.3 3.8 %collective-permute-start.13 = (f32[4,1024]{1,0:T(4,128)S(1)}, f32[4,1024]{1,0:T(4,128)S(1)}, u32[]{:S(2)}, u32[]{:S(2)}) collective-permute-start(f32[4,1024]{1,0:T(4,128)S(1)} %get-tuple-element.94), channel_id=1, source_target_pairs={{0,16},{8,24},{16,0},{24,8},{1,17},{9,25},{17,1},{25,9},{2,18},{10... | collective-permute-start | bytes 49160 | tf_op jit(solution)/shard_map/ppermute | solution.py:631

commit v3 on v2

--- a/solution.py
+++ b/solution.py
@@ -106,10 +106,12 @@
         softmax(1)
 
 
-def places(slots):
+def places(slots, merged=True):
     if slots < 4:
         return [(s, None) for s in range(slots)]
     found = [(0, None), (1, None), (2, 0), (2, 1)]
+    if not merged:
+        return found + [(s - 1, None) for s in range(4, slots)]
     for n in range(3, 3 * slots // 4, 3):
         found += [(n, None), (n + 2, 0), (n + 1, None), (n + 2, 1)]
     return found
@@ -411,21 +413,32 @@
     )(after_this, keys, ds, *so_far)
 
 
-def own_grads(after_this, queries, leaf_keys, own, p, ds):
-    heads = p.shape[0]
-    shape = jax.ShapeDtypeStruct(leaf_keys.shape, jnp.bfloat16)
-    return pl.pallas_call(
-        own_grads_kernel,
-        in_specs=[ANY] + [VMEM] * 6,
-        out_specs=[ANY] * 2,
-        out_shape=[shape] * 2,
-        scratch_shapes=[pltpu.VMEM(shape.shape, shape.dtype)] * 2
-        + [pltpu.SemaphoreType.DMA((heads, 2))],
+def last_grads_kernel(heads_per, first, count, half, after_ref, keys_ref, ds_ref, q0, g0, q1, g1, p_ref, *refs):
+    dq_hbm, dk_hbm, dv_hbm, dq_ref, dk_ref, dv_ref, dq_sems, own_sems = refs[1:]
+    query_grads_kernel(heads_per, first, count, half, after_ref, keys_ref, ds_ref, dq_hbm, dq_ref, dq_sems)
+    own_grads_kernel(after_ref, q0, g0, q1, g1, p_ref, ds_ref, dk_hbm, dv_hbm, dk_ref, dv_ref, own_sems)
+
+
+def last_grads(after_this, first, so_far, leaf_keys, own, keys, p, ds):
+    rows, cols = so_far.shape
+    heads = keys.shape[0]
+    count = heads - first
+    span = cols // heads
+    own_shape = jax.ShapeDtypeStruct(leaf_keys.shape, jnp.bfloat16)
+    return pl.pallas_call(
+        functools.partial(last_grads_kernel, span // HD, first, count, rows // 2),
+        in_specs=[ANY] + [VMEM] * 7 + [ANY],
+        out_specs=[ANY] * 3,
+        out_shape=[jax.ShapeDtypeStruct(so_far.shape, jnp.bfloat16), own_shape, own_shape],
+        input_output_aliases={8: 0},
+        scratch_shapes=[pltpu.VMEM((rows, count * span), jnp.bfloat16)]
+        + [pltpu.VMEM(own_shape.shape, jnp.bfloat16)] * 2
+        + [pltpu.SemaphoreType.DMA(s) for s in ((count,), (heads, 2))],
         compiler_params=pltpu.CompilerParams(
             vmem_limit_bytes=(10 if ds.shape[1] <= 1024 else 52) << 20
         ),
-        cost_estimate=cost(2, leaf_keys.shape[0], queries, 2 * queries.size),
-    )(*in_hbm(after_this), *own[0][:2], *own[1][:2], p, ds)
+        cost_estimate=cost(2, keys.shape[1], so_far, 2 * so_far.size),
+    )(after_this, keys, ds, *own[0][:2], *own[1][:2], p, so_far)
 
 
 def gather_kernel(mk_ref, mv_ref, rk_ref, rv_ref, mid_ref, pair_ref):
@@ -515,7 +528,7 @@
         for s in range(slots)
     ]
     held = {}
-    for s, (i, j) in enumerate(places(slots)):
+    for s, (i, j) in enumerate(places(slots, False)):
         at = mid_rows * (j or 0)
         outs[i][at : at + mid_rows] = mids[s][...]
         held.setdefault(i, []).append(roots[s])
@@ -527,9 +540,9 @@
     slots = len(mids)
     mid_rows, cols = mids[0].shape
     rows = mid_rows + a.shape[0] // slots
-    arrays = arrays_of(slots)
-    paired = {i for i, j in places(slots) if j is not None}
-    shapes = [(2 * rows if i in paired else rows, cols) for i in range(arrays)]
+    found = places(slots, False)
+    paired = {i for i, j in found if j is not None}
+    shapes = [(2 * rows if i in paired else rows, cols) for i in range(found[-1][0] + 1)]
     return pl.pallas_call(
         functools.partial(spread_kernel, slots, mid_rows),
         in_specs=[ANY] + [VMEM] * (2 + slots),
@@ -554,21 +567,17 @@
     )(first, a, pair)
 
 
-def far_sums_kernel(mid_rows, _, a_ref, b_ref, pair_ref, *outs):
-    for j, (x, o) in enumerate(zip((a_ref, b_ref), outs)):
-        mid = pair_ref[j * mid_rows : (j + 1) * mid_rows].astype(jnp.float32)
-        o[:mid_rows] = (x[:mid_rows].astype(jnp.float32) + mid).astype(jnp.bfloat16)
-        root = root_of(x, mid_rows, None) + root_of(pair_ref, mid_rows, j)
-        o[mid_rows:] = root.astype(jnp.bfloat16)
-
-
-def far_sums(first, a, b, pair, mid_rows):
-    return pl.pallas_call(
-        functools.partial(far_sums_kernel, mid_rows),
-        in_specs=[ANY] + [VMEM] * 3,
-        out_shape=[jax.ShapeDtypeStruct(x.shape, x.dtype) for x in (a, b)],
-        compiler_params=pltpu.CompilerParams(vmem_limit_bytes=8 << 20),
-    )(*in_hbm(first), a, b, pair)
+def far_sum_kernel(_, a_ref, b_ref, out_ref):
+    out_ref[...] = (a_ref[...].astype(jnp.float32) + b_ref[...].astype(jnp.float32)).astype(jnp.bfloat16)
+
+
+def far_sum(first, a, b):
+    return pl.pallas_call(
+        far_sum_kernel,
+        in_specs=[ANY] + [VMEM] * 2,
+        out_shape=jax.ShapeDtypeStruct(a.shape, a.dtype),
+        compiler_params=pltpu.CompilerParams(vmem_limit_bytes=4 << 20),
+    )(first, a, b)
 
 
 def mid_sums_kernel(mid_part, *refs):
@@ -679,25 +688,28 @@
     )
 
     heads = leaf_keys.shape[1] // HD
-    cuts = [0, heads // 4, heads]
+    cuts = [0, heads // 4, heads // 2, heads]
 
     def query_part(first, i, so_far):
         return query_grads(first, cuts[i], cuts[i + 1] - cuts[i], so_far, queries, keys, ds)
 
     query_grad = query_part(where, 0, ())
     terms = spread(query_grad, root_terms[0], swap(root_terms[1], "mid", mids, 1), mid_terms)
-    through = {f: leaf_swap(terms[3 * f // 4 + 2], 1) for f in range(4, leaves, 4)}
+    through = [leaf_swap(terms[s], 1) for s in far]
     query_grad = query_part(terms[0], 1, (query_grad,))
+    (token,) = in_hbm(query_grad)
     near = leaf_swap(terms[2], 2) if leaves >= 4 else None
     arrived = [terms[0]] if near is None else [terms[0], near]
     last = terms[0]
-    for f, x in through.items():
-        n = 3 * f // 4
-        a, last = far_sums(query_grad, terms[n], terms[n + 1], x, mid_rows)
-        arrived += [leaf_swap(last, f + 2), leaf_swap(a, f)]
+    for s, x in zip(far, through):
+        last = far_sum(token, terms[s - 1], x)
+        token = last
+        arrived.append(leaf_swap(last, s))
     beside = terms[1] if near is None else near_sum(last, terms[1], near, mid_rows)
     arrived.append(leaf_swap(beside, 1))
-    leaf_key_grad, leaf_value_grad = own_grads(query_grad, queries, leaf_keys, own, own_p, ds)
+    query_grad, leaf_key_grad, leaf_value_grad = last_grads(
+        beside, cuts[2], query_grad, leaf_keys, own, keys, own_p, ds
+    )
     pieces = root_sums(leaf_value_grad, arrived, mid_rows, root_own, mids // 2)
     mid_key_grad, mid_value_grad = mid_sums(arrived, mid_part)
     pieces = [pieces[0]] + [swap(x, "mid", mids, t) for t, x in zip(same_core, pieces[1:])]

time: 53.9 us -> 53.3 us (0.989)
  waiting for transfers between devices: 13 us -> 8.74 us
  starting transfers between devices: 15.4 us -> 18.2 us
  Pallas kernels: 23.2 us -> 23.9 us
    ppermute x14 -> x15, waiting for transfers between devices: 13 us -> 8.74 us  [swap(): return lax.ppermute(x, axis, [(i, i ^ offset) for i in range(size)])]
    ppermute x14 -> x15, starting transfers between devices: 15.4 us -> 18.2 us  [swap(): return lax.ppermute(x, axis, [(i, i ^ offset) for i in range(size)])]
    pallas_call x2 -> x3, Pallas kernels: 3.06 us -> 5.46 us  [the longest x1 5.42 us: last_grads(): pl.pallas_call(functools.partial(last_grads_kernel, span // HD, first, co...]
    pallas_call x2, Pallas kernels: 4.8 us -> 3.11 us  [query_grads(): pl.pallas_call(functools.partial(query_grads_kernel, heads_per, first, co...]
  transfers between devices with their start and end apart: 14 -> 15, of which waited for: 8 -> 6; matrix products, arithmetic and copies ran while one was open for 0% -> 0% of each run, Pallas kernels for 28% -> 29%
where the time goes in v3:
time: 53.3 us; the launch traced here: 53 us
  Pallas kernels  23.9 us (45%)
  starting transfers between devices  18.2 us (34%)
  waiting for transfers between devices  8.74 us (16%)
  between operations  2.1 us (4%)
    ppermute x15, starting transfers between devices, swap(): return lax.ppermute(x, axis, [(i, i ^ offset) for i in range(size)])  18.2 us
    ppermute x15, waiting for transfers between devices, swap(): return lax.ppermute(x, axis, [(i, i ^ offset) for i in range(size)])  8.74 us
    pallas_call x1, Pallas kernels, terms_part(): pl.pallas_call(functools.partial(terms_kernel, slots, mid_part), in_specs...  6.81 us
    pallas_call x2, Pallas kernels, own_part(): pl.pallas_call(functools.partial(own_kernel, parity), in_specs=[ANY] * 5,...  6.27 us
    pallas_call x1, Pallas kernels, last_grads(): pl.pallas_call(functools.partial(last_grads_kernel, span // HD, first, co...  5.42 us
    pallas_call x2, Pallas kernels, query_grads(): pl.pallas_call(functools.partial(query_grads_kernel, heads_per, first, co...  3.11 us
  transfers between devices with their start and end apart: 15, of which 6 were waited for; matrix products, arithmetic and copies ran while one was open for 0% of the time, Pallas kernels for 29%

profile of v3, /device:TPU:0, one launch (start us, length us, event | category | flops | bytes accessed | tf_op | source)
XLA Modules:
  0.0 53.0 jit_solution(13589434657450200423)
XLA Ops:
  0.6 0.8 %shard_map.153 = (bf16[32,1024]{1,0:T(8,128)(2,1)S(1)}, bf16[4,1024]{1,0:T(4,128)(2,1)S(1)}) custom-call(bf16[16,1024]{1,0:T(8,128)(2,1)} %mk_ref.1, bf16[16,1024]{1,0:T(8,128)(2,1)} %mv_ref.1, bf16[2,1024]{1,0:T(2,128)(2,1)} %rk_ref.1, bf16[2,1024]{1,0:T(2,128)(2,1)} %rv_ref.1), custom_call_target="tpu_custom_call" | custom-call | tf_op jit(solution)/shard_map/pallas_call | solution.py:450
  1.4 3.0 %collective-permute-start = (bf16[4,1024]{1,0:T(4,128)(2,1)S(1)}, bf16[4,1024]{1,0:T(4,128)(2,1)S(1)}, u32[]{:S(2)}, u32[]{:S(2)}) collective-permute-start(bf16[4,1024]{1,0:T(4,128)(2,1)S(1)} %get-tuple-element.53.refs_0_), channel_id=1, source_target_pairs={{0,16},{8,24},{16,0},{24,8},{1,17},{9,25},{17,1},{25,9},{2,18},{10... | collective-permute-start | bytes 24584 | tf_op jit(solution)/shard_map/ppermute | solution.py:640
  5.8 0.3 collective-permute-done.refs_1_
  6.1 2.1 %collective-permute-start.3 = (bf16[40,1024]{1,0:T(8,128)(2,1)S(1)}, bf16[40,1024]{1,0:T(8,128)(2,1)S(1)}, u32[]{:S(2)}, u32[]{:S(2)}) collective-permute-start(bf16[40,1024]{1,0:T(8,128)(2,1)S(1)} %shard_map.154._.a_ref.refs_0_.refs_14_), channel_id=1, source_target_pairs={{0,1},{1,0},{2,3},{3,2},{4,5},{5,4},{6,7},{7,6},{8,9},{9,8},{10,11... | collective-permute-start | bytes 245768 | tf_op jit(solution)/shard_map/ppermute | solution.py:640
  8.2 3.6 %collective-permute-start.2 = (bf16[40,1024]{1,0:T(8,128)(2,1)S(1)}, bf16[40,1024]{1,0:T(8,128)(2,1)S(1)}, u32[]{:S(2)}, u32[]{:S(2)}) collective-permute-start(bf16[40,1024]{1,0:T(8,128)(2,1)S(1)} %shard_map.154._.a_ref.refs_0_.refs_14_), channel_id=1, source_target_pairs={{0,6},{1,7},{2,4},{3,5},{4,2},{5,3},{6,0},{7,1},{8,14},{9,15},{10,... | collective-permute-start | bytes 245768 | tf_op jit(solution)/shard_map/ppermute | solution.py:640
  11.8 3.1 %shard_map.155 = (bf16[4,256,512]{2,1,0:T(8,128)(2,1)S(1)}, bf16[4,256,512]{2,1,0:T(8,128)(2,1)S(1)}, bf16[4,256,128]{2,1,0:T(8,128)(2,1)S(1)}, bf16[4,256,128]{...) custom-call(bf16[40,1024]{1,0:T(8,128)(2,1)S(1)} %shard_map.154._.a_ref.r, ...), custom_call_target="tpu_custom_call" | custom-call | flops 536870912 | bytes 2097152 | tf_op jit(solution)/shard_map/pallas_call | solution.py:352
  14.9 0.9 %collective-permute-start.4 = (bf16[80,1024]{1,0:T(8,128)(2,1)S(1)}, bf16[80,1024]{1,0:T(8,128)(2,1)S(1)}, u32[]{:S(2)}, u32[]{:S(2)}) collective-permute-start(bf16[80,1024]{1,0:T(8,128)(2,1)S(1)} %shard_map.158), channel_id=1, source_target_pairs={{0,2},{1,3},{2,0},{3,1},{4,6},{5,7},{6,4},{7,5},{8,10},{9,11},{10,... | collective-permute-start | bytes 491528 | tf_op jit(solution)/shard_map/ppermute | solution.py:640
  15.8 0.0 collective-permute-done.2.b_ref.refs_4_.refs_18_
  15.8 2.0 %collective-permute-done.1.a_ref.refs_3_.refs_17_ = bf16[40,1024]{1,0:T(8,128)(2,1)S(1)} collective-permute-done((bf16[40,1024]{1,0:T(8,128)(2,1)S(1)}, bf16[40,1024]{1,0:T(8,128)(2,1)S(1)}, u32[]{:S(2)}, u32[]{:S(2)}) %collective-permute-start.1) | collective-permute-done | bytes 81952 | tf_op jit(solution)/shard_map/ppermute | solution.py:640
  17.8 0.6 %collective-permute-start.5 = (bf16[80,1024]{1,0:T(8,128)(2,1)S(1)}, bf16[80,1024]{1,0:T(8,128)(2,1)S(1)}, u32[]{:S(2)}, u32[]{:S(2)}) collective-permute-start(bf16[80,1024]{1,0:T(8,128)(2,1)S(1)} %shard_map.156._), channel_id=1, source_target_pairs={{0,1},{1,0},{2,3},{3,2},{4,5},{5,4},{6,7},{7,6},{8,9},{9,8},{10,11... | collective-permute-start | bytes 491528 | tf_op jit(solution)/shard_map/ppermute | solution.py:640
  18.4 3.2 %shard_map.157 = (bf16[4,256,512]{2,1,0:T(8,128)(2,1)S(1)}, bf16[4,256,512]{2,1,0:T(8,128)(2,1)S(1)}, bf16[4,256,128]{2,1,0:T(8,128)(2,1)S(1)}, bf16[4,256,128]{...) custom-call(bf16[80,1024]{1,0:T(8,128)(2,1)S(1)} %shard_map.156._, ...), custom_call_target="tpu_custom_call" | custom-call | flops 536870912 | bytes 2097152 | tf_op jit(solution)/shard_map/pallas_call | solution.py:352
  21.6 1.6 %collective-permute-done.5.refs_5_.refs_19_ = bf16[80,1024]{1,0:T(8,128)(2,1)S(1)} collective-permute-done((bf16[80,1024]{1,0:T(8,128)(2,1)S(1)}, bf16[80,1024]{1,0:T(8,128)(2,1)S(1)}, u32[]{:S(2)}, u32[]{:S(2)}) %collective-permute-start.5) | collective-permute-done | bytes 163872 | tf_op jit(solution)/shard_map/ppermute | solution.py:640
  23.3 0.1 collective-permute-start.6
  23.4 1.3 %collective-permute-done.6.refs_21_ = bf16[64,1024]{1,0:T(8,128)(2,1)S(1)} collective-permute-done((bf16[64,1024]{1,0:T(8,128)(2,1)S(1)}, bf16[64,1024]{1,0:T(8,128)(2,1)S(1)}, u32[]{:S(2)}, u32[]{:S(2)}) %collective-permute-start.6) | collective-permute-done | bytes 131104 | tf_op jit(solution)/shard_map/ppermute | solution.py:640
  24.7 6.8 %shard_map.160 = (bf16[8,448,128]{2,1,0:T(8,128)(2,1)S(1)}, bf16[8,768,512]{2,1,0:T(8,128)(2,1)S(1)}, bf16[8,384,512]{2,1,0:T(8,128)(2,1)S(1)}, bf16[32,1024]{1,...) custom-call(s32[1]{0:T(128)} %bitcast.where_ref._, ...), custom_call_target="tpu_custom_call" | custom-call | flops 3758096384 | bytes 4194304 | tf_op jit(solution)/shard_map/pallas_call | solution.py:378
  31.5 0.2 collective-permute-start.7
  31.7 1.6 %shard_map.161._.refs_0_ = bf16[256,4096]{1,0:T(8,128)(2,1)} custom-call(s32[1]{0:T(128)} %bitcast.where_ref._, bf16[8,448,128]{2,1,0:T(8,128)(2,1)S(1)} %get-tuple-element.68.keys_ref, bf16[8,768,512]{2,1,0:T(8,128)(2,1)S(1)} %get-tuple-element.69.ds_ref), custom_call_target="tpu_custom_call" | custom-call | flops 234881024 | bytes 2097152 | tf_op jit(solution)/shard_map/pallas_call | solution.py:399
  33.3 0.1 shard_map.162
  33.4 0.1 collective-permute-start.10
  33.5 0.6 %collective-permute-start.8 = (bf16[40,1024]{1,0:T(8,128)(2,1)S(1)}, bf16[40,1024]{1,0:T(8,128)(2,1)S(1)}, u32[]{:S(2)}, u32[]{:S(2)}) collective-permute-start(bf16[40,1024]{1,0:T(8,128)(2,1)S(1)} %get-tuple-element.82), channel_id=1, source_target_pairs={{0,1},{1,0},{2,3},{3,2},{4,5},{5,4},{6,7},{7,6},{8,9},{9,8},{10,11... | collective-permute-start | bytes 245768 | tf_op jit(solution)/shard_map/ppermute | solution.py:640
  34.1 1.5 %collective-permute-start.9 = (bf16[40,1024]{1,0:T(8,128)(2,1)S(1)}, bf16[40,1024]{1,0:T(8,128)(2,1)S(1)}, u32[]{:S(2)}, u32[]{:S(2)}) collective-permute-start(bf16[40,1024]{1,0:T(8,128)(2,1)S(1)} %get-tuple-element.84), channel_id=1, source_target_pairs={{0,1},{1,0},{2,3},{3,2},{4,5},{5,4},{6,7},{7,6},{8,9},{9,8},{10,11... | collective-permute-start | bytes 245768 | tf_op jit(solution)/shard_map/ppermute | solution.py:640
  35.6 1.6 %shard_map.163._.refs_0_ = bf16[256,4096]{1,0:T(8,128)(2,1)} custom-call(bf16[40,1024]{1,0:T(8,128)(2,1)S(1)} %get-tuple-element.80._.refs_0_, bf16[8,448,128]{2,1,0:T(8,128)(2,1)S(1)} %get-tuple-element.68.keys_ref, bf16[8,768,512]{2,1,0:T(8,128)(2,1)S(1)} %get-tuple-element.69.ds_ref, ...), custom_call_target="tpu_custom_call", output_to_operand_aliasing={{}: (3, {})} | custom-call | flops 234881024 | bytes 2097152 | tf_op jit(solution)/shard_map/pallas_call | solution.py:399
  37.2 1.7 %collective-permute-done.8.b_ref = bf16[40,1024]{1,0:T(8,128)(2,1)S(1)} collective-permute-done((bf16[40,1024]{1,0:T(8,128)(2,1)S(1)}, bf16[40,1024]{1,0:T(8,128)(2,1)S(1)}, u32[]{:S(2)}, u32[]{:S(2)}) %collective-permute-start.8) | collective-permute-done | bytes 81952 | tf_op jit(solution)/shard_map/ppermute | solution.py:640
  38.9 2.5 %collective-permute-start.11 = (bf16[40,1024]{1,0:T(8,128)(2,1)S(1)}, bf16[40,1024]{1,0:T(8,128)(2,1)S(1)}, u32[]{:S(2)}, u32[]{:S(2)}) collective-permute-start(bf16[40,1024]{1,0:T(8,128)(2,1)S(1)} %shard_map.164._), channel_id=1, source_target_pairs={{0,6},{1,7},{2,4},{3,5},{4,2},{5,3},{6,0},{7,1},{8,14},{9,15},{10,... | collective-permute-start | bytes 245768 | tf_op jit(solution)/shard_map/ppermute | solution.py:640
  41.3 0.0 collective-permute-done.9.b_ref
  41.4 1.1 %collective-permute-start.12 = (bf16[40,1024]{1,0:T(8,128)(2,1)S(1)}, bf16[40,1024]{1,0:T(8,128)(2,1)S(1)}, u32[]{:S(2)}, u32[]{:S(2)}) collective-permute-start(bf16[40,1024]{1,0:T(8,128)(2,1)S(1)} %shard_map.165._), channel_id=1, source_target_pairs={{0,4},{1,5},{2,6},{3,7},{4,0},{5,1},{6,2},{7,3},{8,12},{9,13},{10,... | collective-permute-start | bytes 245768 | tf_op jit(solution)/shard_map/ppermute | solution.py:640
  42.5 0.6 %collective-permute-start.13 = (bf16[40,1024]{1,0:T(8,128)(2,1)S(1)}, bf16[40,1024]{1,0:T(8,128)(2,1)S(1)}, u32[]{:S(2)}, u32[]{:S(2)}) collective-permute-start(bf16[40,1024]{1,0:T(8,128)(2,1)S(1)} %shard_map.166.after_ref), channel_id=1, source_target_pairs={{0,1},{1,0},{2,3},{3,2},{4,5},{5,4},{6,7},{7,6},{8,9},{9,8},{10,11... | collective-permute-start | bytes 245768 | tf_op jit(solution)/shard_map/ppermute | solution.py:640
  43.1 5.4 %shard_map.167 = (bf16[256,4096]{1,0:T(8,128)(2,1)}, bf16[256,1024]{1,0:T(8,128)(2,1)}, bf16[256,1024]{1,0:T(8,128)(2,1)}) custom-call(bf16[40,1024]{1,0:T(8,128)(2,1)S(1)} %shard_map.166.after_ref, bf16[8,448,128]{2,1,0:T(8,128)(2,1)S(1)} %get-tuple-element.68.keys_ref, ...), custom_call_target="tpu_custom_call", output_to_operand_aliasing={{0}: (8, {})} | custom-call | flops 1879048192 | bytes 2097152 | tf_op jit(solution)/shard_map/pallas_call | solution.py:428
  48.6 1.4 %collective-permute-start.14 = (f32[4,1024]{1,0:T(4,128)S(1)}, f32[4,1024]{1,0:T(4,128)S(1)}, u32[]{:S(2)}, u32[]{:S(2)}) collective-permute-start(f32[4,1024]{1,0:T(4,128)S(1)} %get-tuple-element.94), channel_id=1, source_target_pairs={{0,16},{8,24},{16,0},{24,8},{1,17},{9,25},{17,1},{25,9},{2,18},{10... | collective-permute-start | bytes 49160 | tf_op jit(solution)/shard_map/ppermute | solution.py:640
  50.0 0.7 %shard_map.168 = (f32[16,1024]{1,0:T(8,128)}, f32[16,1024]{1,0:T(8,128)}) custom-call(bf16[40,1024]{1,0:T(8,128)(2,1)S(1)} %get-tuple-element.80._.refs_0_, bf16[80,1024]{1,0:T(8,128)(2,1)S(1)} %collective-permute-done.10.pair_ref.refs_1_, bf16[40,1024]{1,0:T(8,128)(2,1)S(1)} %collective-permute-done.11.refs_2_, ...), custom_call_target="tpu_custom_call" | custom-call | tf_op jit(solution)/shard_map/pallas_call | solution.py:593
  50.7 1.7 %collective-permute-done.14.refs_1_ = f32[4,1024]{1,0:T(4,128)S(1)} collective-permute-done((f32[4,1024]{1,0:T(4,128)S(1)}, f32[4,1024]{1,0:T(4,128)S(1)}, u32[]{:S(2)}, u32[]{:S(2)}) %collective-permute-start.14) | collective-permute-done | bytes 16416 | tf_op jit(solution)/shard_map/ppermute | solution.py:640
  52.4 0.6 %shard_map.170 = (f32[2,1024]{1,0:T(2,128)}, f32[2,1024]{1,0:T(2,128)}) custom-call(f32[4,1024]{1,0:T(4,128)S(1)} %get-tuple-element.93.refs_0_, f32[4,1024]{1,0:T(4,128)S(1)} %collective-permute-done.14.refs_1_), custom_call_target="tpu_custom_call" | custom-call | tf_op jit(solution)/shard_map/pallas_call | solution.py:632
  (16 shorter events, 0.2 us)
Async XLA Ops:
  1.4 4.7 %collective-permute-start = (bf16[4,1024]{1,0:T(4,128)(2,1)S(1)}, bf16[4,1024]{1,0:T(4,128)(2,1)S(1)}, u32[]{:S(2)}, u32[]{:S(2)}) collective-permute-start(bf16[4,1024]{1,0:T(4,128)(2,1)S(1)} %get-tuple-element.53.refs_0_), channel_id=1, source_target_pairs={{0,16},{8,24},{16,0},{24,8},{1,17},{9,25},{17,1},{25,9},{2,18},{10... | collective-permute-start | bytes 24584 | tf_op jit(solution)/shard_map/ppermute | solution.py:640
  6.1 8.8 %collective-permute-start.3 = (bf16[40,1024]{1,0:T(8,128)(2,1)S(1)}, bf16[40,1024]{1,0:T(8,128)(2,1)S(1)}, u32[]{:S(2)}, u32[]{:S(2)}) collective-permute-start(bf16[40,1024]{1,0:T(8,128)(2,1)S(1)} %shard_map.154._.a_ref.refs_0_.refs_14_), channel_id=1, source_target_pairs={{0,1},{1,0},{2,3},{3,2},{4,5},{5,4},{6,7},{7,6},{8,9},{9,8},{10,11... | collective-permute-start | bytes 245768 | tf_op jit(solution)/shard_map/ppermute | solution.py:640
  8.2 7.6 %collective-permute-start.2 = (bf16[40,1024]{1,0:T(8,128)(2,1)S(1)}, bf16[40,1024]{1,0:T(8,128)(2,1)S(1)}, u32[]{:S(2)}, u32[]{:S(2)}) collective-permute-start(bf16[40,1024]{1,0:T(8,128)(2,1)S(1)} %shard_map.154._.a_ref.refs_0_.refs_14_), channel_id=1, source_target_pairs={{0,6},{1,7},{2,4},{3,5},{4,2},{5,3},{6,0},{7,1},{8,14},{9,15},{10,... | collective-permute-start | bytes 245768 | tf_op jit(solution)/shard_map/ppermute | solution.py:640
  11.8 6.0 %collective-permute-start.1 = (bf16[40,1024]{1,0:T(8,128)(2,1)S(1)}, bf16[40,1024]{1,0:T(8,128)(2,1)S(1)}, u32[]{:S(2)}, u32[]{:S(2)}) collective-permute-start(bf16[40,1024]{1,0:T(8,128)(2,1)S(1)} %shard_map.154._.a_ref.refs_0_.refs_14_), channel_id=1, source_target_pairs={{0,4},{1,5},{2,6},{3,7},{4,0},{5,1},{6,2},{7,3},{8,12},{9,13},{10,... | collective-permute-start | bytes 245768 | tf_op jit(solution)/shard_map/ppermute | solution.py:640
  14.9 6.7 %collective-permute-start.4 = (bf16[80,1024]{1,0:T(8,128)(2,1)S(1)}, bf16[80,1024]{1,0:T(8,128)(2,1)S(1)}, u32[]{:S(2)}, u32[]{:S(2)}) collective-permute-start(bf16[80,1024]{1,0:T(8,128)(2,1)S(1)} %shard_map.158), channel_id=1, source_target_pairs={{0,2},{1,3},{2,0},{3,1},{4,6},{5,7},{6,4},{7,5},{8,10},{9,11},{10,... | collective-permute-start | bytes 491528 | tf_op jit(solution)/shard_map/ppermute | solution.py:640
  17.8 5.4 %collective-permute-start.5 = (bf16[80,1024]{1,0:T(8,128)(2,1)S(1)}, bf16[80,1024]{1,0:T(8,128)(2,1)S(1)}, u32[]{:S(2)}, u32[]{:S(2)}) collective-permute-start(bf16[80,1024]{1,0:T(8,128)(2,1)S(1)} %shard_map.156._), channel_id=1, source_target_pairs={{0,1},{1,0},{2,3},{3,2},{4,5},{5,4},{6,7},{7,6},{8,9},{9,8},{10,11... | collective-permute-start | bytes 491528 | tf_op jit(solution)/shard_map/ppermute | solution.py:640
  23.3 1.4 %collective-permute-start.6 = (bf16[64,1024]{1,0:T(8,128)(2,1)S(1)}, bf16[64,1024]{1,0:T(8,128)(2,1)S(1)}, u32[]{:S(2)}, u32[]{:S(2)}) collective-permute-start(bf16[64,1024]{1,0:T(8,128)(2,1)S(1)} %shard_map.159.refs_20_), channel_id=1, source_target_pairs={{0,8},{8,0},{16,24},{24,16},{1,9},{9,1},{17,25},{25,17},{2,10},{10... | collective-permute-start | bytes 393224 | tf_op jit(solution)/shard_map/ppermute | solution.py:640
  31.5 1.8 %collective-permute-start.7 = (bf16[64,1024]{1,0:T(8,128)(2,1)S(1)}, bf16[64,1024]{1,0:T(8,128)(2,1)S(1)}, u32[]{:S(2)}, u32[]{:S(2)}) collective-permute-start(bf16[64,1024]{1,0:T(8,128)(2,1)S(1)} %get-tuple-element.71), channel_id=1, source_target_pairs={{0,8},{8,0},{16,24},{24,16},{1,9},{9,1},{17,25},{25,17},{2,10},{10... | collective-permute-start | bytes 393224 | tf_op jit(solution)/shard_map/ppermute | solution.py:640
  33.4 9.1 %collective-permute-start.10 = (bf16[80,1024]{1,0:T(8,128)(2,1)S(1)}, bf16[80,1024]{1,0:T(8,128)(2,1)S(1)}, u32[]{:S(2)}, u32[]{:S(2)}) collective-permute-start(bf16[80,1024]{1,0:T(8,128)(2,1)S(1)} %get-tuple-element.86), channel_id=1, source_target_pairs={{0,2},{1,3},{2,0},{3,1},{4,6},{5,7},{6,4},{7,5},{8,10},{9,11},{10,... | collective-permute-start | bytes 491528 | tf_op jit(solution)/shard_map/ppermute | solution.py:640
  33.5 5.3 %collective-permute-start.8 = (bf16[40,1024]{1,0:T(8,128)(2,1)S(1)}, bf16[40,1024]{1,0:T(8,128)(2,1)S(1)}, u32[]{:S(2)}, u32[]{:S(2)}) collective-permute-start(bf16[40,1024]{1,0:T(8,128)(2,1)S(1)} %get-tuple-element.82), channel_id=1, source_target_pairs={{0,1},{1,0},{2,3},{3,2},{4,5},{5,4},{6,7},{7,6},{8,9},{9,8},{10,11... | collective-permute-start | bytes 245768 | tf_op jit(solution)/shard_map/ppermute | solution.py:640
  34.1 7.3 %collective-permute-start.9 = (bf16[40,1024]{1,0:T(8,128)(2,1)S(1)}, bf16[40,1024]{1,0:T(8,128)(2,1)S(1)}, u32[]{:S(2)}, u32[]{:S(2)}) collective-permute-start(bf16[40,1024]{1,0:T(8,128)(2,1)S(1)} %get-tuple-element.84), channel_id=1, source_target_pairs={{0,1},{1,0},{2,3},{3,2},{4,5},{5,4},{6,7},{7,6},{8,9},{9,8},{10,11... | collective-permute-start | bytes 245768 | tf_op jit(solution)/shard_map/ppermute | solution.py:640
  38.9 9.7 %collective-permute-start.11 = (bf16[40,1024]{1,0:T(8,128)(2,1)S(1)}, bf16[40,1024]{1,0:T(8,128)(2,1)S(1)}, u32[]{:S(2)}, u32[]{:S(2)}) collective-permute-start(bf16[40,1024]{1,0:T(8,128)(2,1)S(1)} %shard_map.164._), channel_id=1, source_target_pairs={{0,6},{1,7},{2,4},{3,5},{4,2},{5,3},{6,0},{7,1},{8,14},{9,15},{10,... | collective-permute-start | bytes 245768 | tf_op jit(solution)/shard_map/ppermute | solution.py:640
  41.4 7.2 %collective-permute-start.12 = (bf16[40,1024]{1,0:T(8,128)(2,1)S(1)}, bf16[40,1024]{1,0:T(8,128)(2,1)S(1)}, u32[]{:S(2)}, u32[]{:S(2)}) collective-permute-start(bf16[40,1024]{1,0:T(8,128)(2,1)S(1)} %shard_map.165._), channel_id=1, source_target_pairs={{0,4},{1,5},{2,6},{3,7},{4,0},{5,1},{6,2},{7,3},{8,12},{9,13},{10,... | collective-permute-start | bytes 245768 | tf_op jit(solution)/shard_map/ppermute | solution.py:640
  42.5 6.1 %collective-permute-start.13 = (bf16[40,1024]{1,0:T(8,128)(2,1)S(1)}, bf16[40,1024]{1,0:T(8,128)(2,1)S(1)}, u32[]{:S(2)}, u32[]{:S(2)}) collective-permute-start(bf16[40,1024]{1,0:T(8,128)(2,1)S(1)} %shard_map.166.after_ref), channel_id=1, source_target_pairs={{0,1},{1,0},{2,3},{3,2},{4,5},{5,4},{6,7},{7,6},{8,9},{9,8},{10,11... | collective-permute-start | bytes 245768 | tf_op jit(solution)/shard_map/ppermute | solution.py:640
  48.6 3.8 %collective-permute-start.14 = (f32[4,1024]{1,0:T(4,128)S(1)}, f32[4,1024]{1,0:T(4,128)S(1)}, u32[]{:S(2)}, u32[]{:S(2)}) collective-permute-start(f32[4,1024]{1,0:T(4,128)S(1)} %get-tuple-element.94), channel_id=1, source_target_pairs={{0,16},{8,24},{16,0},{24,8},{1,17},{9,25},{17,1},{25,9},{2,18},{10... | collective-permute-start | bytes 49160 | tf_op jit(solution)/shard_map/ppermute | solution.py:640

commit v4 on v3

--- a/solution.py
+++ b/solution.py
@@ -258,7 +258,7 @@
         b.finish()
 
 
-def query_grads_kernel(heads_per, first, count, half, _, keys_ref, ds_ref, *refs):
+def query_grads_kernel(heads_per, first, count, half, finish, _, keys_ref, ds_ref, *refs):
     dq_hbm, dq_ref, sems = refs[-3:]
     n_all = keys_ref.shape[1]
     span = heads_per * HD
@@ -282,8 +282,17 @@
                 dq_ref[part * half : (part + 1) * half, at] = dq[g * half : (g + 1) * half]
         copy_out(i).start()
 
-    for i in range(count):
-        copy_out(i).wait()
+    def wait():
+        for i in range(count):
+            copy_out(i).wait()
+
+    if finish:
+        wait()
+    return wait
+
+
+def run_query_grads(heads_per, first, count, half, *refs):
+    query_grads_kernel(heads_per, first, count, half, True, *refs)
 
 
 def own_grads_kernel(_, q0_ref, g0_ref, q1_ref, g1_ref, p_ref, ds_ref, dk_hbm, dv_hbm, dk_ref, dv_ref, sems):
@@ -397,7 +406,7 @@
     heads = keys.shape[0]
     heads_per = cols // (heads * HD)
     return pl.pallas_call(
-        functools.partial(query_grads_kernel, heads_per, first, count, rows // 2),
+        functools.partial(run_query_grads, heads_per, first, count, rows // 2),
         in_specs=[ANY] + [VMEM] * 2 + [ANY] * len(so_far),
         out_specs=ANY,
         out_shape=jax.ShapeDtypeStruct(queries.shape, jnp.bfloat16),
@@ -415,8 +424,11 @@
 
 def last_grads_kernel(heads_per, first, count, half, after_ref, keys_ref, ds_ref, q0, g0, q1, g1, p_ref, *refs):
     dq_hbm, dk_hbm, dv_hbm, dq_ref, dk_ref, dv_ref, dq_sems, own_sems = refs[1:]
-    query_grads_kernel(heads_per, first, count, half, after_ref, keys_ref, ds_ref, dq_hbm, dq_ref, dq_sems)
+    wait = query_grads_kernel(
+        heads_per, first, count, half, False, after_ref, keys_ref, ds_ref, dq_hbm, dq_ref, dq_sems
+    )
     own_grads_kernel(after_ref, q0, g0, q1, g1, p_ref, ds_ref, dk_hbm, dv_hbm, dk_ref, dv_ref, own_sems)
+    wait()
 
 
 def last_grads(after_this, first, so_far, leaf_keys, own, keys, p, ds):
@@ -688,7 +700,7 @@
     )
 
     heads = leaf_keys.shape[1] // HD
-    cuts = [0, heads // 4, heads // 2, heads]
+    cuts = [0, heads // 4, heads * 5 // 8, heads]
 
     def query_part(first, i, so_far):
         return query_grads(first, cuts[i], cuts[i + 1] - cuts[i], so_far, queries, keys, ds)

time: 53.3 us -> 53.1 us (level)
  Pallas kernels: 23.9 us -> 23.2 us
    pallas_call x1, Pallas kernels: 5.42 us -> 4.27 us  [last_grads(): pl.pallas_call(functools.partial(last_grads_kernel, span // HD, first, co...]
  transfers between devices with their start and end apart: 15 -> 15, of which waited for: 6 -> 7; matrix products, arithmetic and copies ran while one was open for 0% -> 0% of each run, Pallas kernels for 29% -> 28%
where the time goes in v4:
time: 53.1 us; the launch traced here: 52.9 us
  Pallas kernels  23.2 us (44%)
  starting transfers between devices  18.3 us (34%)
  waiting for transfers between devices  9.24 us (17%)
  between operations  2.08 us (4%)
    ppermute x15, starting transfers between devices, swap(): return lax.ppermute(x, axis, [(i, i ^ offset) for i in range(size)])  18.3 us
    ppermute x15, waiting for transfers between devices, swap(): return lax.ppermute(x, axis, [(i, i ^ offset) for i in range(size)])  9.24 us
    pallas_call x1, Pallas kernels, terms_part(): pl.pallas_call(functools.partial(terms_kernel, slots, mid_part), in_specs...  6.81 us
    pallas_call x2, Pallas kernels, own_part(): pl.pallas_call(functools.partial(own_kernel, parity), in_specs=[ANY] * 5,...  6.27 us
    pallas_call x1, Pallas kernels, last_grads(): pl.pallas_call(functools.partial(last_grads_kernel, span // HD, first, co...  4.27 us
    pallas_call x2, Pallas kernels, query_grads(): pl.pallas_call(functools.partial(run_query_grads, heads_per, first, count...  3.51 us
  transfers between devices with their start and end apart: 15, of which 7 were waited for; matrix products, arithmetic and copies ran while one was open for 0% of the time, Pallas kernels for 28%

profile of v4, /device:TPU:0, one launch (start us, length us, event | category | flops | bytes accessed | tf_op | source)
XLA Modules:
  0.0 52.9 jit_solution(17015849591975244416)
XLA Ops:
  0.6 0.8 %shard_map.153 = (bf16[32,1024]{1,0:T(8,128)(2,1)S(1)}, bf16[4,1024]{1,0:T(4,128)(2,1)S(1)}) custom-call(bf16[16,1024]{1,0:T(8,128)(2,1)} %mk_ref.1, bf16[16,1024]{1,0:T(8,128)(2,1)} %mv_ref.1, bf16[2,1024]{1,0:T(2,128)(2,1)} %rk_ref.1, bf16[2,1024]{1,0:T(2,128)(2,1)} %rv_ref.1), custom_call_target="tpu_custom_call" | custom-call | tf_op jit(solution)/shard_map/pallas_call | solution.py:462
  1.4 3.0 %collective-permute-start = (bf16[4,1024]{1,0:T(4,128)(2,1)S(1)}, bf16[4,1024]{1,0:T(4,128)(2,1)S(1)}, u32[]{:S(2)}, u32[]{:S(2)}) collective-permute-start(bf16[4,1024]{1,0:T(4,128)(2,1)S(1)} %get-tuple-element.53.refs_0_), channel_id=1, source_target_pairs={{0,16},{8,24},{16,0},{24,8},{1,17},{9,25},{17,1},{25,9},{2,18},{10... | collective-permute-start | bytes 24584 | tf_op jit(solution)/shard_map/ppermute | solution.py:652
  5.8 0.3 collective-permute-done.refs_1_
  6.1 2.1 %collective-permute-start.3 = (bf16[40,1024]{1,0:T(8,128)(2,1)S(1)}, bf16[40,1024]{1,0:T(8,128)(2,1)S(1)}, u32[]{:S(2)}, u32[]{:S(2)}) collective-permute-start(bf16[40,1024]{1,0:T(8,128)(2,1)S(1)} %shard_map.154._.a_ref.refs_0_.refs_14_), channel_id=1, source_target_pairs={{0,1},{1,0},{2,3},{3,2},{4,5},{5,4},{6,7},{7,6},{8,9},{9,8},{10,11... | collective-permute-start | bytes 245768 | tf_op jit(solution)/shard_map/ppermute | solution.py:652
  8.2 3.6 %collective-permute-start.2 = (bf16[40,1024]{1,0:T(8,128)(2,1)S(1)}, bf16[40,1024]{1,0:T(8,128)(2,1)S(1)}, u32[]{:S(2)}, u32[]{:S(2)}) collective-permute-start(bf16[40,1024]{1,0:T(8,128)(2,1)S(1)} %shard_map.154._.a_ref.refs_0_.refs_14_), channel_id=1, source_target_pairs={{0,6},{1,7},{2,4},{3,5},{4,2},{5,3},{6,0},{7,1},{8,14},{9,15},{10,... | collective-permute-start | bytes 245768 | tf_op jit(solution)/shard_map/ppermute | solution.py:652
  11.8 0.0 collective-permute-start.1
  11.8 3.1 %shard_map.155 = (bf16[4,256,512]{2,1,0:T(8,128)(2,1)S(1)}, bf16[4,256,512]{2,1,0:T(8,128)(2,1)S(1)}, bf16[4,256,128]{2,1,0:T(8,128)(2,1)S(1)}, bf16[4,256,128]{...) custom-call(bf16[40,1024]{1,0:T(8,128)(2,1)S(1)} %shard_map.154._.a_ref.r, ...), custom_call_target="tpu_custom_call" | custom-call | flops 536870912 | bytes 2097152 | tf_op jit(solution)/shard_map/pallas_call | solution.py:361
  14.9 0.9 %collective-permute-start.4 = (bf16[80,1024]{1,0:T(8,128)(2,1)S(1)}, bf16[80,1024]{1,0:T(8,128)(2,1)S(1)}, u32[]{:S(2)}, u32[]{:S(2)}) collective-permute-start(bf16[80,1024]{1,0:T(8,128)(2,1)S(1)} %shard_map.158), channel_id=1, source_target_pairs={{0,2},{1,3},{2,0},{3,1},{4,6},{5,7},{6,4},{7,5},{8,10},{9,11},{10,... | collective-permute-start | bytes 491528 | tf_op jit(solution)/shard_map/ppermute | solution.py:652
  15.8 2.0 %collective-permute-done.1.a_ref.refs_3_.refs_17_ = bf16[40,1024]{1,0:T(8,128)(2,1)S(1)} collective-permute-done((bf16[40,1024]{1,0:T(8,128)(2,1)S(1)}, bf16[40,1024]{1,0:T(8,128)(2,1)S(1)}, u32[]{:S(2)}, u32[]{:S(2)}) %collective-permute-start.1) | collective-permute-done | bytes 81952 | tf_op jit(solution)/shard_map/ppermute | solution.py:652
  17.8 0.6 %collective-permute-start.5 = (bf16[80,1024]{1,0:T(8,128)(2,1)S(1)}, bf16[80,1024]{1,0:T(8,128)(2,1)S(1)}, u32[]{:S(2)}, u32[]{:S(2)}) collective-permute-start(bf16[80,1024]{1,0:T(8,128)(2,1)S(1)} %shard_map.156._), channel_id=1, source_target_pairs={{0,1},{1,0},{2,3},{3,2},{4,5},{5,4},{6,7},{7,6},{8,9},{9,8},{10,11... | collective-permute-start | bytes 491528 | tf_op jit(solution)/shard_map/ppermute | solution.py:652
  18.4 3.2 %shard_map.157 = (bf16[4,256,512]{2,1,0:T(8,128)(2,1)S(1)}, bf16[4,256,512]{2,1,0:T(8,128)(2,1)S(1)}, bf16[4,256,128]{2,1,0:T(8,128)(2,1)S(1)}, bf16[4,256,128]{...) custom-call(bf16[80,1024]{1,0:T(8,128)(2,1)S(1)} %shard_map.156._, ...), custom_call_target="tpu_custom_call" | custom-call | flops 536870912 | bytes 2097152 | tf_op jit(solution)/shard_map/pallas_call | solution.py:361
  21.6 1.6 %collective-permute-done.5.refs_5_.refs_19_ = bf16[80,1024]{1,0:T(8,128)(2,1)S(1)} collective-permute-done((bf16[80,1024]{1,0:T(8,128)(2,1)S(1)}, bf16[80,1024]{1,0:T(8,128)(2,1)S(1)}, u32[]{:S(2)}, u32[]{:S(2)}) %collective-permute-start.5) | collective-permute-done | bytes 163872 | tf_op jit(solution)/shard_map/ppermute | solution.py:652
  23.3 0.1 collective-permute-start.6
  23.4 1.3 %collective-permute-done.6.refs_21_ = bf16[64,1024]{1,0:T(8,128)(2,1)S(1)} collective-permute-done((bf16[64,1024]{1,0:T(8,128)(2,1)S(1)}, bf16[64,1024]{1,0:T(8,128)(2,1)S(1)}, u32[]{:S(2)}, u32[]{:S(2)}) %collective-permute-start.6) | collective-permute-done | bytes 131104 | tf_op jit(solution)/shard_map/ppermute | solution.py:652
  24.7 6.8 %shard_map.160 = (bf16[8,448,128]{2,1,0:T(8,128)(2,1)S(1)}, bf16[8,768,512]{2,1,0:T(8,128)(2,1)S(1)}, bf16[8,384,512]{2,1,0:T(8,128)(2,1)S(1)}, bf16[32,1024]{1,...) custom-call(s32[1]{0:T(128)} %bitcast.where_ref.refs_0_, ...), custom_call_target="tpu_custom_call" | custom-call | flops 3758096384 | bytes 4194304 | tf_op jit(solution)/shard_map/pallas_call | solution.py:387
  31.5 0.2 collective-permute-start.7
  31.7 1.6 %shard_map.161._.refs_3_ = bf16[256,4096]{1,0:T(8,128)(2,1)} custom-call(s32[1]{0:T(128)} %bitcast.where_ref.refs_0_, bf16[8,448,128]{2,1,0:T(8,128)(2,1)S(1)} %get-tuple-element.68.refs_1_.keys_ref, bf16[8,768,512]{2,1,0:T(8,128)(2,1)S(1)} %get-tuple-element.69.refs_2_.ds_ref), custom_call_target="tpu_custom_call" | custom-call | flops 234881024 | bytes 2097152 | tf_op jit(solution)/shard_map/pallas_call | solution.py:408
  33.3 0.1 shard_map.162
  33.4 0.1 collective-permute-start.10
  33.5 0.6 %collective-permute-start.8 = (bf16[40,1024]{1,0:T(8,128)(2,1)S(1)}, bf16[40,1024]{1,0:T(8,128)(2,1)S(1)}, u32[]{:S(2)}, u32[]{:S(2)}) collective-permute-start(bf16[40,1024]{1,0:T(8,128)(2,1)S(1)} %get-tuple-element.82), channel_id=1, source_target_pairs={{0,1},{1,0},{2,3},{3,2},{4,5},{5,4},{6,7},{7,6},{8,9},{9,8},{10,11... | collective-permute-start | bytes 245768 | tf_op jit(solution)/shard_map/ppermute | solution.py:652
  34.1 1.5 %collective-permute-start.9 = (bf16[40,1024]{1,0:T(8,128)(2,1)S(1)}, bf16[40,1024]{1,0:T(8,128)(2,1)S(1)}, u32[]{:S(2)}, u32[]{:S(2)}) collective-permute-start(bf16[40,1024]{1,0:T(8,128)(2,1)S(1)} %get-tuple-element.84), channel_id=1, source_target_pairs={{0,1},{1,0},{2,3},{3,2},{4,5},{5,4},{6,7},{7,6},{8,9},{9,8},{10,11... | collective-permute-start | bytes 245768 | tf_op jit(solution)/shard_map/ppermute | solution.py:652
  35.6 2.0 %shard_map.163._.refs_0_ = bf16[256,4096]{1,0:T(8,128)(2,1)} custom-call(bf16[40,1024]{1,0:T(8,128)(2,1)S(1)} %get-tuple-element.80.refs_0_, bf16[8,448,128]{2,1,0:T(8,128)(2,1)S(1)} %get-tuple-element.68.refs_1_.keys_ref, bf16[8,768,512]{2,1,0:T(8,128)(2,1)S(1)} %get-tuple-element.69.refs_2_.ds_ref, ...), custom_call_target="tpu_custom_call", output_to_operand_aliasing={{}: (3, {})} | custom-call | flops 352321536 | bytes 2097152 | tf_op jit(solution)/shard_map/pallas_call | solution.py:408
  37.6 1.3 %collective-permute-done.8.b_ref = bf16[40,1024]{1,0:T(8,128)(2,1)S(1)} collective-permute-done((bf16[40,1024]{1,0:T(8,128)(2,1)S(1)}, bf16[40,1024]{1,0:T(8,128)(2,1)S(1)}, u32[]{:S(2)}, u32[]{:S(2)}) %collective-permute-start.8) | collective-permute-done | bytes 81952 | tf_op jit(solution)/shard_map/ppermute | solution.py:652
  38.9 2.5 %collective-permute-start.11 = (bf16[40,1024]{1,0:T(8,128)(2,1)S(1)}, bf16[40,1024]{1,0:T(8,128)(2,1)S(1)}, u32[]{:S(2)}, u32[]{:S(2)}) collective-permute-start(bf16[40,1024]{1,0:T(8,128)(2,1)S(1)} %shard_map.164._), channel_id=1, source_target_pairs={{0,6},{1,7},{2,4},{3,5},{4,2},{5,3},{6,0},{7,1},{8,14},{9,15},{10,... | collective-permute-start | bytes 245768 | tf_op jit(solution)/shard_map/ppermute | solution.py:652
  41.4 1.1 %collective-permute-start.12 = (bf16[40,1024]{1,0:T(8,128)(2,1)S(1)}, bf16[40,1024]{1,0:T(8,128)(2,1)S(1)}, u32[]{:S(2)}, u32[]{:S(2)}) collective-permute-start(bf16[40,1024]{1,0:T(8,128)(2,1)S(1)} %shard_map.165._), channel_id=1, source_target_pairs={{0,4},{1,5},{2,6},{3,7},{4,0},{5,1},{6,2},{7,3},{8,12},{9,13},{10,... | collective-permute-start | bytes 245768 | tf_op jit(solution)/shard_map/ppermute | solution.py:652
  42.5 0.6 %collective-permute-start.13 = (bf16[40,1024]{1,0:T(8,128)(2,1)S(1)}, bf16[40,1024]{1,0:T(8,128)(2,1)S(1)}, u32[]{:S(2)}, u32[]{:S(2)}) collective-permute-start(bf16[40,1024]{1,0:T(8,128)(2,1)S(1)} %shard_map.166.after_ref), channel_id=1, source_target_pairs={{0,1},{1,0},{2,3},{3,2},{4,5},{5,4},{6,7},{7,6},{8,9},{9,8},{10,11... | collective-permute-start | bytes 245768 | tf_op jit(solution)/shard_map/ppermute | solution.py:652
  43.1 4.3 %shard_map.167 = (bf16[256,4096]{1,0:T(8,128)(2,1)}, bf16[256,1024]{1,0:T(8,128)(2,1)}, bf16[256,1024]{1,0:T(8,128)(2,1)}) custom-call(bf16[40,1024]{1,0:T(8,128)(2,1)S(1)} %shard_map.166.after_ref, bf16[8,448,128]{2,1,0:T(8,128)(2,1)S(1)} %get-tuple-element.68.refs_1_.keys_ref, ...), custom_call_target="tpu_custom_call", output_to_operand_aliasing={{0}: (8, {})} | custom-call | flops 1879048192 | bytes 2097152 | tf_op jit(solution)/shard_map/pallas_call | solution.py:440
  47.4 1.0 %collective-permute-done.12.refs_3_ = bf16[40,1024]{1,0:T(8,128)(2,1)S(1)} collective-permute-done((bf16[40,1024]{1,0:T(8,128)(2,1)S(1)}, bf16[40,1024]{1,0:T(8,128)(2,1)S(1)}, u32[]{:S(2)}, u32[]{:S(2)}) %collective-permute-start.12) | collective-permute-done | bytes 81952 | tf_op jit(solution)/shard_map/ppermute | solution.py:652
  48.4 1.5 %collective-permute-start.14 = (f32[4,1024]{1,0:T(4,128)S(1)}, f32[4,1024]{1,0:T(4,128)S(1)}, u32[]{:S(2)}, u32[]{:S(2)}) collective-permute-start(f32[4,1024]{1,0:T(4,128)S(1)} %get-tuple-element.94), channel_id=1, source_target_pairs={{0,16},{8,24},{16,0},{24,8},{1,17},{9,25},{17,1},{25,9},{2,18},{10... | collective-permute-start | bytes 49160 | tf_op jit(solution)/shard_map/ppermute | solution.py:652
  50.0 0.7 %shard_map.168 = (f32[16,1024]{1,0:T(8,128)}, f32[16,1024]{1,0:T(8,128)}) custom-call(bf16[40,1024]{1,0:T(8,128)(2,1)S(1)} %get-tuple-element.80.refs_0_, bf16[80,1024]{1,0:T(8,128)(2,1)S(1)} %collective-permute-done.10.pair_ref.refs_1_, bf16[40,1024]{1,0:T(8,128)(2,1)S(1)} %collective-permute-done.11.refs_2_, ...), custom_call_target="tpu_custom_call" | custom-call | tf_op jit(solution)/shard_map/pallas_call | solution.py:605
  50.7 1.6 %collective-permute-done.14.refs_1_ = f32[4,1024]{1,0:T(4,128)S(1)} collective-permute-done((f32[4,1024]{1,0:T(4,128)S(1)}, f32[4,1024]{1,0:T(4,128)S(1)}, u32[]{:S(2)}, u32[]{:S(2)}) %collective-permute-start.14) | collective-permute-done | bytes 16416 | tf_op jit(solution)/shard_map/ppermute | solution.py:652
  52.3 0.6 %shard_map.170 = (f32[2,1024]{1,0:T(2,128)}, f32[2,1024]{1,0:T(2,128)}) custom-call(f32[4,1024]{1,0:T(4,128)S(1)} %get-tuple-element.93.refs_0_, f32[4,1024]{1,0:T(4,128)S(1)} %collective-permute-done.14.refs_1_), custom_call_target="tpu_custom_call" | custom-call | tf_op jit(solution)/shard_map/pallas_call | solution.py:644
  (16 shorter events, 0.2 us)
Async XLA Ops:
  1.4 4.7 %collective-permute-start = (bf16[4,1024]{1,0:T(4,128)(2,1)S(1)}, bf16[4,1024]{1,0:T(4,128)(2,1)S(1)}, u32[]{:S(2)}, u32[]{:S(2)}) collective-permute-start(bf16[4,1024]{1,0:T(4,128)(2,1)S(1)} %get-tuple-element.53.refs_0_), channel_id=1, source_target_pairs={{0,16},{8,24},{16,0},{24,8},{1,17},{9,25},{17,1},{25,9},{2,18},{10... | collective-permute-start | bytes 24584 | tf_op jit(solution)/shard_map/ppermute | solution.py:652
  6.1 8.8 %collective-permute-start.3 = (bf16[40,1024]{1,0:T(8,128)(2,1)S(1)}, bf16[40,1024]{1,0:T(8,128)(2,1)S(1)}, u32[]{:S(2)}, u32[]{:S(2)}) collective-permute-start(bf16[40,1024]{1,0:T(8,128)(2,1)S(1)} %shard_map.154._.a_ref.refs_0_.refs_14_), channel_id=1, source_target_pairs={{0,1},{1,0},{2,3},{3,2},{4,5},{5,4},{6,7},{7,6},{8,9},{9,8},{10,11... | collective-permute-start | bytes 245768 | tf_op jit(solution)/shard_map/ppermute | solution.py:652
  8.2 7.6 %collective-permute-start.2 = (bf16[40,1024]{1,0:T(8,128)(2,1)S(1)}, bf16[40,1024]{1,0:T(8,128)(2,1)S(1)}, u32[]{:S(2)}, u32[]{:S(2)}) collective-permute-start(bf16[40,1024]{1,0:T(8,128)(2,1)S(1)} %shard_map.154._.a_ref.refs_0_.refs_14_), channel_id=1, source_target_pairs={{0,6},{1,7},{2,4},{3,5},{4,2},{5,3},{6,0},{7,1},{8,14},{9,15},{10,... | collective-permute-start | bytes 245768 | tf_op jit(solution)/shard_map/ppermute | solution.py:652
  11.8 6.0 %collective-permute-start.1 = (bf16[40,1024]{1,0:T(8,128)(2,1)S(1)}, bf16[40,1024]{1,0:T(8,128)(2,1)S(1)}, u32[]{:S(2)}, u32[]{:S(2)}) collective-permute-start(bf16[40,1024]{1,0:T(8,128)(2,1)S(1)} %shard_map.154._.a_ref.refs_0_.refs_14_), channel_id=1, source_target_pairs={{0,4},{1,5},{2,6},{3,7},{4,0},{5,1},{6,2},{7,3},{8,12},{9,13},{10,... | collective-permute-start | bytes 245768 | tf_op jit(solution)/shard_map/ppermute | solution.py:652
  14.9 6.7 %collective-permute-start.4 = (bf16[80,1024]{1,0:T(8,128)(2,1)S(1)}, bf16[80,1024]{1,0:T(8,128)(2,1)S(1)}, u32[]{:S(2)}, u32[]{:S(2)}) collective-permute-start(bf16[80,1024]{1,0:T(8,128)(2,1)S(1)} %shard_map.158), channel_id=1, source_target_pairs={{0,2},{1,3},{2,0},{3,1},{4,6},{5,7},{6,4},{7,5},{8,10},{9,11},{10,... | collective-permute-start | bytes 491528 | tf_op jit(solution)/shard_map/ppermute | solution.py:652
  17.8 5.4 %collective-permute-start.5 = (bf16[80,1024]{1,0:T(8,128)(2,1)S(1)}, bf16[80,1024]{1,0:T(8,128)(2,1)S(1)}, u32[]{:S(2)}, u32[]{:S(2)}) collective-permute-start(bf16[80,1024]{1,0:T(8,128)(2,1)S(1)} %shard_map.156._), channel_id=1, source_target_pairs={{0,1},{1,0},{2,3},{3,2},{4,5},{5,4},{6,7},{7,6},{8,9},{9,8},{10,11... | collective-permute-start | bytes 491528 | tf_op jit(solution)/shard_map/ppermute | solution.py:652
  23.3 1.4 %collective-permute-start.6 = (bf16[64,1024]{1,0:T(8,128)(2,1)S(1)}, bf16[64,1024]{1,0:T(8,128)(2,1)S(1)}, u32[]{:S(2)}, u32[]{:S(2)}) collective-permute-start(bf16[64,1024]{1,0:T(8,128)(2,1)S(1)} %shard_map.159.refs_20_), channel_id=1, source_target_pairs={{0,8},{8,0},{16,24},{24,16},{1,9},{9,1},{17,25},{25,17},{2,10},{10... | collective-permute-start | bytes 393224 | tf_op jit(solution)/shard_map/ppermute | solution.py:652
  31.5 1.8 %collective-permute-start.7 = (bf16[64,1024]{1,0:T(8,128)(2,1)S(1)}, bf16[64,1024]{1,0:T(8,128)(2,1)S(1)}, u32[]{:S(2)}, u32[]{:S(2)}) collective-permute-start(bf16[64,1024]{1,0:T(8,128)(2,1)S(1)} %get-tuple-element.71), channel_id=1, source_target_pairs={{0,8},{8,0},{16,24},{24,16},{1,9},{9,1},{17,25},{25,17},{2,10},{10... | collective-permute-start | bytes 393224 | tf_op jit(solution)/shard_map/ppermute | solution.py:652
  33.4 9.1 %collective-permute-start.10 = (bf16[80,1024]{1,0:T(8,128)(2,1)S(1)}, bf16[80,1024]{1,0:T(8,128)(2,1)S(1)}, u32[]{:S(2)}, u32[]{:S(2)}) collective-permute-start(bf16[80,1024]{1,0:T(8,128)(2,1)S(1)} %get-tuple-element.86), channel_id=1, source_target_pairs={{0,2},{1,3},{2,0},{3,1},{4,6},{5,7},{6,4},{7,5},{8,10},{9,11},{10,... | collective-permute-start | bytes 491528 | tf_op jit(solution)/shard_map/ppermute | solution.py:652
  33.5 5.3 %collective-permute-start.8 = (bf16[40,1024]{1,0:T(8,128)(2,1)S(1)}, bf16[40,1024]{1,0:T(8,128)(2,1)S(1)}, u32[]{:S(2)}, u32[]{:S(2)}) collective-permute-start(bf16[40,1024]{1,0:T(8,128)(2,1)S(1)} %get-tuple-element.82), channel_id=1, source_target_pairs={{0,1},{1,0},{2,3},{3,2},{4,5},{5,4},{6,7},{7,6},{8,9},{9,8},{10,11... | collective-permute-start | bytes 245768 | tf_op jit(solution)/shard_map/ppermute | solution.py:652
  34.1 7.3 %collective-permute-start.9 = (bf16[40,1024]{1,0:T(8,128)(2,1)S(1)}, bf16[40,1024]{1,0:T(8,128)(2,1)S(1)}, u32[]{:S(2)}, u32[]{:S(2)}) collective-permute-start(bf16[40,1024]{1,0:T(8,128)(2,1)S(1)} %get-tuple-element.84), channel_id=1, source_target_pairs={{0,1},{1,0},{2,3},{3,2},{4,5},{5,4},{6,7},{7,6},{8,9},{9,8},{10,11... | collective-permute-start | bytes 245768 | tf_op jit(solution)/shard_map/ppermute | solution.py:652
  38.9 8.5 %collective-permute-start.11 = (bf16[40,1024]{1,0:T(8,128)(2,1)S(1)}, bf16[40,1024]{1,0:T(8,128)(2,1)S(1)}, u32[]{:S(2)}, u32[]{:S(2)}) collective-permute-start(bf16[40,1024]{1,0:T(8,128)(2,1)S(1)} %shard_map.164._), channel_id=1, source_target_pairs={{0,6},{1,7},{2,4},{3,5},{4,2},{5,3},{6,0},{7,1},{8,14},{9,15},{10,... | collective-permute-start | bytes 245768 | tf_op jit(solution)/shard_map/ppermute | solution.py:652
  41.4 7.1 %collective-permute-start.12 = (bf16[40,1024]{1,0:T(8,128)(2,1)S(1)}, bf16[40,1024]{1,0:T(8,128)(2,1)S(1)}, u32[]{:S(2)}, u32[]{:S(2)}) collective-permute-start(bf16[40,1024]{1,0:T(8,128)(2,1)S(1)} %shard_map.165._), channel_id=1, source_target_pairs={{0,4},{1,5},{2,6},{3,7},{4,0},{5,1},{6,2},{7,3},{8,12},{9,13},{10,... | collective-permute-start | bytes 245768 | tf_op jit(solution)/shard_map/ppermute | solution.py:652
  42.5 5.9 %collective-permute-start.13 = (bf16[40,1024]{1,0:T(8,128)(2,1)S(1)}, bf16[40,1024]{1,0:T(8,128)(2,1)S(1)}, u32[]{:S(2)}, u32[]{:S(2)}) collective-permute-start(bf16[40,1024]{1,0:T(8,128)(2,1)S(1)} %shard_map.166.after_ref), channel_id=1, source_target_pairs={{0,1},{1,0},{2,3},{3,2},{4,5},{5,4},{6,7},{7,6},{8,9},{9,8},{10,11... | collective-permute-start | bytes 245768 | tf_op jit(solution)/shard_map/ppermute | solution.py:652
  48.4 3.8 %collective-permute-start.14 = (f32[4,1024]{1,0:T(4,128)S(1)}, f32[4,1024]{1,0:T(4,128)S(1)}, u32[]{:S(2)}, u32[]{:S(2)}) collective-permute-start(f32[4,1024]{1,0:T(4,128)S(1)} %get-tuple-element.94), channel_id=1, source_target_pairs={{0,16},{8,24},{16,0},{24,8},{1,17},{9,25},{17,1},{25,9},{2,18},{10... | collective-permute-start | bytes 49160 | tf_op jit(solution)/shard_map/ppermute | solution.py:652
